TPU v7x, 32 devices: a whole 2x2x4 slice. The times are simulated.
32 devices in a mesh: groups: 2 (over y), dev: 16 (over z, x, core).
Axes of the slice: x: 2, y: 2, z: 4, core: 2. Of those that a mesh axis runs over, the one named last changes fastest.
Arguments:
- volumes: bfloat16 [256, 262144], P(('groups', 'dev')), parts along dimension 0, may hold values from -6 to 6
- rotations: bfloat16 [3, 1024, 1024], replicated, may hold values from -0.1875 to 0.1875
- turn_ids: int32 [256], P(('groups', 'dev')), parts along dimension 0, may hold values from 0 to 2
- shifts: int32 [256, 3], P(('groups', 'dev')), parts along dimension 0, may hold values from -4 to 4
- defocus: float32 [256], P(('groups', 'dev')), parts along dimension 0, may hold values from 0.05 to 0.5
- labels: int32 [256], P(('groups', 'dev')), parts along dimension 0, may hold values from 0 to 47
- references: bfloat16 [96, 65536], P('groups', 'dev'), parts along dimension 0, may hold values from -6 to 6
Outputs:
- new_refs: float32 [96, 65536], P('groups', 'dev'), parts along dimension 0
- scores: float32 [256], P(('groups', 'dev')), parts along dimension 0
There are 2 independent parts, one for each index of `groups`. A program takes and returns all parts, laid end to end along the dimension named above; an argument that names none is the same for every part. Nothing has to cross between parts.
All inputs are finite; a program needn't handle non-finite values.
Results may differ from a plain program's by a relative error of at most 0.0069.
Values may be sent and summed in bfloat16 or wider, within the bound.
A program may use at most 128 MiB of HBM per device.

v0:
```python
import math

import jax
import jax.numpy as jnp
from jax import lax
from jax.sharding import PartitionSpec as P

BOX = 64
BAND = 32


TWO_PI = 2.0 * math.pi


def dft_tables():
    sample = jnp.arange(BOX, dtype=jnp.int32)
    frequency = jnp.arange(BAND, dtype=jnp.int32) - BAND // 2
    phase_index = jnp.mod(sample[:, None] * frequency[None, :], BOX).astype(jnp.float32)
    phase_angle = phase_index * (TWO_PI / BOX)
    norm_scale = 1.0 / math.sqrt(BOX)
    cosine = (jnp.cos(phase_angle) * norm_scale).astype(jnp.bfloat16)
    sine_part = (jnp.sin(phase_angle) * norm_scale).astype(jnp.bfloat16)
    first_table = jnp.concatenate([cosine, -sine_part], axis=1)
    mixing = jnp.stack([jnp.stack([cosine, sine_part]), jnp.stack([-sine_part, cosine])])
    return (first_table, mixing)


def transform(volumes):
    particle_count = volumes.shape[0]
    first_table, mixing = dft_tables()
    section_z = jnp.dot(volumes.reshape(-1, BOX), first_table, preferred_element_type=jnp.float32)
    section_z = section_z.astype(jnp.bfloat16).reshape(particle_count, BOX, BOX, 2, BAND)
    section_y = jnp.einsum(
        "pxybz,abyj->pxjaz", section_z, mixing, preferred_element_type=jnp.float32
    ).astype(jnp.bfloat16)
    section_x = jnp.einsum(
        "pxkbz,abxj->pjkaz", section_y, mixing, preferred_element_type=jnp.float32
    ).astype(jnp.bfloat16)
    return section_x.reshape(particle_count, BAND * BAND, 2 * BAND)


def band_grid(cell_count):
    cell_index = jnp.arange(cell_count, dtype=jnp.int32)
    freq_x = cell_index // BAND - BAND // 2
    freq_y = cell_index % BAND - BAND // 2
    freq_z = jnp.arange(BAND, dtype=jnp.int32) - BAND // 2
    return (freq_x[:, None], freq_y[:, None], freq_z[None, :])


def contrast(defocus, freq_x, freq_y, freq_z):
    radius = (freq_x * freq_x + freq_y * freq_y + freq_z * freq_z).astype(jnp.float32)
    return jnp.sin(defocus[:, None, None] * radius[None] / BAND + 0.3)


def weigh_spectra(spectrum, turn_ids, shifts, defocus, rotations):
    particle_count = spectrum.shape[0]
    taken = rotations[turn_ids]
    turned = jnp.einsum("pmn,pnc->pmc", taken, spectrum, preferred_element_type=jnp.float32)
    freq_x, freq_y, freq_z = band_grid(BAND * BAND)
    shift_dot = (
        freq_x[None] * shifts[:, 0, None, None]
        + freq_y[None] * shifts[:, 1, None, None]
        + freq_z[None] * shifts[:, 2, None, None]
    )
    phase_angle = jnp.mod(shift_dot, BOX).astype(jnp.float32) * (TWO_PI / BOX)
    cosine = jnp.cos(phase_angle)
    sine_part = jnp.sin(phase_angle)
    real_part = turned[:, :, :BAND]
    imag_part = turned[:, :, BAND:]
    weight = contrast(defocus, freq_x, freq_y, freq_z)
    aligned = jnp.concatenate(
        [
            weight * (real_part * cosine - imag_part * sine_part),
            weight * (real_part * sine_part + imag_part * cosine),
        ],
        axis=2,
    )
    return (
        aligned.astype(jnp.bfloat16).reshape(particle_count, -1),
        (weight * weight).reshape(particle_count, -1),
    )


def wiener(class_sum, weight_sum):
    class_count, column_count = class_sum.shape
    cell_count = weight_sum.shape[1] // BAND
    filtered = class_sum.reshape(class_count, cell_count, 2, BAND) / (
        weight_sum.reshape(class_count, cell_count, 1, BAND) + 1.0
    )
    return filtered.reshape(class_count, column_count)


def on_device(volumes, rotations, turn_ids, shifts, defocus, labels, references):
    class_count = references.shape[0]
    spectrum = transform(volumes)
    aligned, squared = weigh_spectra(spectrum, turn_ids, shifts, defocus, rotations)
    class_range = jnp.arange(class_count, dtype=jnp.int32)
    everything = lax.all_gather(references, "dev", axis=1, tiled=True)
    member = labels[:, None] == class_range[None, :]
    chosen = jnp.dot(member.astype(jnp.bfloat16), everything, preferred_element_type=jnp.float32)
    wide_rows = aligned.astype(jnp.float32)
    agreement = jnp.sum(wide_rows * chosen, axis=1)
    energy = jnp.sum(wide_rows * wide_rows, axis=1)
    class_part = jnp.dot(member.astype(jnp.bfloat16).T, aligned, preferred_element_type=jnp.float32)
    weight_part = jnp.dot(
        member.astype(jnp.float32).T,
        squared,
        preferred_element_type=jnp.float32,
        precision=lax.Precision.HIGHEST,
    )
    class_sum, weight_sum = (
        lax.psum_scatter(class_part, "dev", scatter_dimension=1, tiled=True),
        lax.psum_scatter(weight_part, "dev", scatter_dimension=1, tiled=True),
    )
    scores = agreement / jnp.sqrt(energy + 1e-06)
    return (wiener(class_sum, weight_sum), scores)


def solution(mesh):
    return jax.shard_map(
        on_device,
        mesh=mesh,
        in_specs=(
            P(("groups", "dev"), None),
            P(),
            P(("groups", "dev")),
            P(("groups", "dev"), None),
            P(("groups", "dev")),
            P(("groups", "dev")),
            P("groups", "dev"),
        ),
        out_specs=(P("groups", "dev"), P(("groups", "dev"))),
        check_vma=False,
    )
```

profile of v0, /device:TPU:0, one launch (start us, length us, event | category | flops | bytes accessed | tf_op | source)
XLA Modules:
  0.0 313.9 jit_solution(5310171152624534748)
XLA Ops:
  7.2 0.0 reduce-scatter.5.cloned.1.call-start
  7.2 0.2 add.207
  7.4 0.2 add.208
  7.6 0.2 add.209
  7.8 8.1 %fusion.21 = f32[48,32768]{1,0:T(8,128)} fusion(f32[32768]{0:T(1024)S(1)} %add_convert_fusion, f32[8]{0:T(128)} %param.11, s32[8]{0:T(128)} %param.12), kind=kOutput, calls=%fused_computation.30 | convolution fusion | flops 152043904 | bytes 6422592 | tf_op jit(solution)/shard_map/dot_general | solution.py:105
  15.9 0.0 reduce-scatter.5.cloned.1.call-update
  15.9 0.0 all-gather.2.cloned.1.call-start
  16.0 0.7 all-gather.2.cloned.1.call-update
  16.7 0.0 reduce-scatter.3.cloned.1.call-start
  16.7 6.1 %reshape.396 = bf16[2097152]{0:T(1024)(128)(2,1)} reshape(bf16[8,262144]{1,0:T(8,128)(2,1)} %param.7) | data formatting | bytes 8388608
  22.8 11.3 %reshape.370 = bf16[32768,64]{1,0:T(8,128)(2,1)} reshape(bf16[2097152]{0:T(1024)(128)(2,1)} %reshape.396) | data formatting | bytes 8388608 | tf_op jit(solution)/shard_map/reshape | solution.py:31
  34.1 0.2 fusion.48
  34.3 0.1 multiply_convert_fusion.1
  34.4 9.0 %fusion = bf16[32768,64]{0,1:T(8,128)(2,1)} fusion(bf16[32768,64]{1,0:T(8,128)(2,1)} %reshape.370, bf16[64,32]{0,1:T(8,128)(2,1)S(1)} %fusion.48, bf16[64,32]{0,1:T(8,128)(2,1)S(1)} %multiply_convert_fusion.1), kind=kOutput, calls=%fused_computation.4 | convolution fusion | flops 270548992 | bytes 8396800 | tf_op jit(solution)/shard_map/dot_general | solution.py:31
  43.4 11.5 %reshape.371 = bf16[8,64,64,2,32]{2,1,0,4,3:T(8,128)(2,1)} reshape(bf16[32768,64]{0,1:T(8,128)(2,1)} %fusion) | data formatting | bytes 8388608 | tf_op jit(solution)/shard_map/reshape | solution.py:32
  54.9 0.1 fusion.62
  55.0 0.2 multiply_convert_fusion.2
  55.2 7.5 %fusion.8 = bf16[8,64,32,2,32]{1,2,4,0,3:T(8,128)(2,1)S(1)} fusion(bf16[8,64,64,2,32]{2,1,0,4,3:T(8,128)(2,1)} %reshape.371, bf16[1,2,64,32]{2,3,1,0:T(8,128)(2,1)S(1)} %get-tuple-element.9, bf16[1,2,64,32]{2,3,1,0:T(8,128)(2,1)S(1)} %get-tuple-element.8), kind=kOutput, calls=%fused_computation.14 | convolution fusion | flops 269516800 | bytes 6307840 | tf_op jit(solution)/shard_map/pxybz,abyj->pxjaz/dot_general | solution.py:33
  62.7 5.4 %fusion.9 = bf16[8,32,32,2,32]{4,1,2,0,3:T(8,128)(2,1)} fusion(bf16[8,64,32,2,32]{1,2,4,0,3:T(8,128)(2,1)S(1)} %fusion.8, bf16[1,2,64,32]{2,3,1,0:T(8,128)(2,1)S(1)} %get-tuple-element.9, bf16[1,2,64,32]{2,3,1,0:T(8,128)(2,1)S(1)} %get-tuple-element.8), kind=kOutput, calls=%fused_computation.15 | convolution fusion | flops 134774784 | bytes 3162112 | tf_op jit(solution)/shard_map/pxkbz,abxj->pjkaz/dot_general | solution.py:36
  68.2 10.9 %copy.16 = bf16[8,32,32,2,32]{2,1,4,3,0:T(8,128)(2,1)} copy(bf16[8,32,32,2,32]{4,1,2,0,3:T(8,128)(2,1)} %fusion.9) | data formatting | bytes 2097152 | tf_op jit(solution)/shard_map/convert_element_type | solution.py:38
  79.1 7.0 %reshape.372 = bf16[8,1024,64]{1,2,0:T(8,128)(2,1)} reshape(bf16[8,32,32,2,32]{2,1,4,3,0:T(8,128)(2,1)} %copy.16) | data formatting | bytes 2097152 | tf_op jit(solution)/shard_map/reshape | solution.py:39
  86.1 0.0 copy-done.4
  86.1 5.9 %fusion.70 = (bf16[3,512,1024]{2,1,0:T(8,128)(2,1)}, bf16[3,512,1024]{2,1,0:T(8,128)(2,1)S(1)}) fusion(bf16[3,1024,1024]{2,1,0:T(8,128)(2,1)} %param.8), kind=kLoop, calls=%fused_computation.113 | loop fusion | bytes 12582912 | tf_op jit(solution)/shard_map/gather | solution.py:57
  92.0 6.5 %gather_fusion = bf16[8,512,1024]{2,1,0:T(8,128)(2,1)} fusion(bf16[3,512,1024]{2,1,0:T(8,128)(2,1)} %get-tuple-element.4, s32[1024]{0:T(1024)S(1)} %pad_clamp_fusion), kind=kCustom, calls=%fused_computation | custom fusion | bytes 16777248 | tf_op jit(solution)/shard_map/gather | solution.py:57
  98.5 4.5 %gather_fusion.1 = bf16[8,512,1024]{2,1,0:T(8,128)(2,1)} fusion(bf16[3,512,1024]{2,1,0:T(8,128)(2,1)S(1)} %get-tuple-element.5, s32[1024]{0:T(1024)S(1)} %pad_clamp_fusion), kind=kCustom, calls=%fused_computation.1 | custom fusion | bytes 16777248 | tf_op jit(solution)/shard_map/gather | solution.py:57
  103.0 0.0 copy-done.3
  103.0 0.1 broadcast_multiply_fusion
  103.1 0.1 multiply_add_fusion
  103.1 0.1 add_convert_fusion.1
  103.2 0.0 copy-start.2
  103.2 8.9 %fusion.1 = f32[8,1024,64]{1,2,0:T(8,128)S(1)} fusion(bf16[8,1024,64]{1,2,0:T(8,128)(2,1)} %reshape.372, bf16[8,512,1024]{2,1,0:T(8,128)(2,1)} %gather_fusion.1, bf16[8,512,1024]{2,1,0:T(8,128)(2,1)} %gather_fusion), kind=kOutput, calls=%fused_computation.5 | convolution fusion | flops 1107296256 | bytes 19922944 | tf_op jit(solution)/shard_map/pmn,pnc->pmc/dot_general | solution.py:58
  112.1 0.0 copy-start.1
  112.1 8.2 %subtract_multiply_fusion = (bf16[8,1024,32]{1,2,0:T(8,128)(2,1)S(1)}, bf16[8,1024,32]{1,2,0:T(8,128)(2,1)S(1)}) fusion(f32[8,1024,64]{1,2,0:T(8,128)S(1)} %fusion.1, s32[8,32]{1,0:T(8,128)S(1)} %broadcast_multiply_fusion, s32[8,1024]{1,0:T(8,128)S(1)} %multiply_add_fusion, f32[1024,32]{0,1:T(8,128)S(1)} %add_convert_fusion.1, f32[8]{0:T(128)S(1)} %copy-done.2), kind=kLoop, calls=%fused_computation.37 | loop fusion | flops 7077888 | bytes 3310624 | tf_op jit(solution)/shard_map/mul | solution.py:73
  120.4 0.3 multiply_reduce_fusion
  120.7 1.1 copy.17
  121.8 1.5 convert_element_type.123
  123.3 6.4 %fusion.58 = f32[48,65536]{1,0:T(8,128)} fusion(bf16[8,65536]{1,0:T(8,128)(2,1)S(1)} %convert_element_type.123, s32[8]{0:T(128)S(1)} %copy-done.1), kind=kOutput, calls=%fused_computation.94 | convolution fusion | flops 50332032 | bytes 13631520 | tf_op jit(solution)/shard_map/dot_general | solution.py:104
  129.7 0.0 reduce-scatter.3.cloned.1.call-update
  129.7 0.0 reduce-scatter.5.cloned.1.call-done
  129.8 1.0 broadcast_add_fusion
  130.8 1.4 copy.24
  132.2 1.5 div.42
  133.7 1.5 copy.20
  135.1 32.1 %all-gather.2.cloned.1.call-done = bf16[48,65536]{1,0:T(8,128)(2,1)} async-done(((bf16[48,4096]{1,0:T(8,128)(2,1)}), bf16[48,65536]{1,0:T(8,128)(2,1)}) %all-gather.2.cloned.1.call-update) | async-done | bytes 6291472 | tf_op jit(solution)/shard_map/all_gather | solution.py:98
  167.3 3.9 %fusion.17 = f32[8]{0:T(128)S(1)} fusion(bf16[48,65536]{1,0:T(8,128)(2,1)} %all-gather.2.cloned.1.call-done, bf16[8,65536]{1,0:T(8,128)(2,1)S(1)} %convert_element_type.123, s32[8]{0:T(128)S(1)} %copy-done.1), kind=kOutput, calls=%fused_computation.26 | convolution fusion | flops 51904888 | bytes 7340096 | tf_op jit(solution)/shard_map/dot_general | solution.py:100
  171.2 0.5 rsqrt_multiply_fusion
  171.7 133.6 %reduce-scatter.3.cloned.1.call-done = f32[48,4096]{1,0:T(8,128)} async-done(((f32[48,65536]{1,0:T(8,128)}), f32[48,4096]{1,0:T(8,128)}) %reduce-scatter.3.cloned.1.call-update) | async-done | bytes 786448 | tf_op jit(solution)/shard_map/reduce_scatter | solution.py:112
  305.3 2.1 div.44
  (16 shorter events, 0.1 us)
Async XLA Ops:
  7.2 122.6 %reduce-scatter.5.cloned.1.call-start = ((), (), s32[]{:S(2)}) async-start(), calls=%async_computation.3 | async-start | bytes 6684672 | tf_op jit(solution)/shard_map/reduce_scatter | solution.py:113
  15.9 151.4 %all-gather.2.cloned.1.call-start = ((), (), s32[]{:S(2)}) async-start(), calls=%async_computation.4 | async-start | bytes 6684672 | tf_op jit(solution)/shard_map/all_gather | solution.py:98
  16.7 288.6 %reduce-scatter.3.cloned.1.call-start = ((), (), s32[]{:S(2)}) async-start(), calls=%async_computation.2 | async-start | bytes 13369344 | tf_op jit(solution)/shard_map/reduce_scatter | solution.py:112
  68.2 17.9 %copy-start.4 = (s32[8]{0:T(128)S(1)}, s32[8]{0:T(128)}, u32[]{:S(2)}) copy-start(s32[8]{0:T(128)} %param.9) | copy-start | bytes 100
  98.5 4.5 %copy-start.3 = (s32[8,3]{0,1:T(4,128)S(1)}, s32[8,3]{0,1:T(4,128)}, u32[]{:S(2)}) copy-start(s32[8,3]{0,1:T(4,128)} %param.10) | copy-start | bytes 292
  103.2 8.9 %copy-start.2 = (f32[8]{0:T(128)S(1)}, f32[8]{0:T(128)}, u32[]{:S(2)}) copy-start(f32[8]{0:T(128)} %param.11) | copy-start | bytes 100
  112.1 11.2 %copy-start.1 = (s32[8]{0:T(128)S(1)}, s32[8]{0:T(128)}, u32[]{:S(2)}) copy-start(s32[8]{0:T(128)} %param.12) | copy-start | bytes 100
  135.1 170.1 %copy-start = (f32[48,4096]{1,0:T(8,128)S(1)}, f32[48,4096]{1,0:T(8,128)}, u32[]{:S(2)}) copy-start(f32[48,4096]{1,0:T(8,128)} %copy.20) | copy-start | bytes 2359300
Sparse Core Ops, SparseCore 0:
  16.0 87.8 reduce-scatter.4
  106.4 60.8 all-gather.1
  171.9 133.3 reduce-scatter.2
where the time goes:
time: 315 us; the launch traced here: 314 us
  waiting for transfers between devices  166 us (53%)
  local copies, waits for them, and re-layouts  71.1 us (23%)
  matrix products  49.2 us (16%)
  between operations  13.9 us (4%)
  other arithmetic  13.1 us (4%)
    reduce_scatter x1, waiting for transfers between devices, on_device(): lax.psum_scatter(class_part, 'dev', scatter_dimension=1, tiled=True)  134 us
    all_gather x1, waiting for transfers between devices, on_device(): everything = lax.all_gather(references, 'dev', axis=1, tiled=True)  32.1 us
    gather x3, local copies, waits for them, and re-layouts, weigh_spectra(): taken = rotations[turn_ids]  16.9 us
    reshape x1, local copies, waits for them, and re-layouts, transform(): section_z.astype(jnp.bfloat16).reshape(particle_count, BOX, BOX, 2, BAND)  11.5 us
    reshape x1, local copies, waits for them, and re-layouts, transform(): volumes.reshape(-1, BOX)  11.3 us
    convert_element_type x1, local copies, waits for them, and re-layouts, transform(): section_x = jnp.einsum('pxkbz,abxj->pjkaz', section_y, mixing, preferred_...  10.9 us
    dot_general x1, matrix products, transform(): jnp.dot(volumes.reshape(-1, BOX), first_table, preferred_element_type=jnp...  9 us
    dot_general x1, matrix products, weigh_spectra(): jnp.einsum('pmn,pnc->pmc', taken, spectrum, preferred_element_type=jnp.fl...  8.87 us
  transfers between devices with their start and end apart: 3, of which 2 were waited for; matrix products, arithmetic and copies ran while one was open for 39% of the time, Pallas kernels for 0%

commit v1 on v0

--- a/solution.py
+++ b/solution.py
@@ -39,8 +39,8 @@
     return section_x.reshape(particle_count, BAND * BAND, 2 * BAND)
 
 
-def band_grid(cell_count):
-    cell_index = jnp.arange(cell_count, dtype=jnp.int32)
+def band_grid(cell_count, first_cell=0):
+    cell_index = first_cell + jnp.arange(cell_count, dtype=jnp.int32)
     freq_x = cell_index // BAND - BAND // 2
     freq_y = cell_index % BAND - BAND // 2
     freq_z = jnp.arange(BAND, dtype=jnp.int32) - BAND // 2
@@ -75,10 +75,7 @@
         ],
         axis=2,
     )
-    return (
-        aligned.astype(jnp.bfloat16).reshape(particle_count, -1),
-        (weight * weight).reshape(particle_count, -1),
-    )
+    return aligned.astype(jnp.bfloat16).reshape(particle_count, -1)
 
 
 def wiener(class_sum, weight_sum):
@@ -91,27 +88,30 @@
 
 
 def on_device(volumes, rotations, turn_ids, shifts, defocus, labels, references):
-    class_count = references.shape[0]
+    class_count, column_count = references.shape
+    cell_count = column_count // (2 * BAND)
     spectrum = transform(volumes)
-    aligned, squared = weigh_spectra(spectrum, turn_ids, shifts, defocus, rotations)
-    class_range = jnp.arange(class_count, dtype=jnp.int32)
-    everything = lax.all_gather(references, "dev", axis=1, tiled=True)
-    member = labels[:, None] == class_range[None, :]
-    chosen = jnp.dot(member.astype(jnp.bfloat16), everything, preferred_element_type=jnp.float32)
+    aligned = weigh_spectra(spectrum, turn_ids, shifts, defocus, rotations)
     wide_rows = aligned.astype(jnp.float32)
-    agreement = jnp.sum(wide_rows * chosen, axis=1)
     energy = jnp.sum(wide_rows * wide_rows, axis=1)
-    class_part = jnp.dot(member.astype(jnp.bfloat16).T, aligned, preferred_element_type=jnp.float32)
-    weight_part = jnp.dot(
+    facts = jnp.stack([labels.astype(jnp.float32), defocus])
+    facts = lax.all_gather(facts, "dev", axis=1, tiled=True)
+    held = lax.all_to_all(aligned, "dev", split_axis=1, concat_axis=0, tiled=True)
+    member = facts[0][:, None] == jnp.arange(class_count, dtype=jnp.float32)[None, :]
+    table = member.astype(jnp.bfloat16)
+    freq_x, freq_y, freq_z = band_grid(cell_count, lax.axis_index("dev") * cell_count)
+    weight = contrast(facts[1], freq_x, freq_y, freq_z)
+    squared = (weight * weight).reshape(facts.shape[1], -1)
+    class_sum = jnp.dot(table.T, held, preferred_element_type=jnp.float32)
+    weight_sum = jnp.dot(
         member.astype(jnp.float32).T,
         squared,
         preferred_element_type=jnp.float32,
         precision=lax.Precision.HIGHEST,
     )
-    class_sum, weight_sum = (
-        lax.psum_scatter(class_part, "dev", scatter_dimension=1, tiled=True),
-        lax.psum_scatter(weight_part, "dev", scatter_dimension=1, tiled=True),
-    )
+    chosen = jnp.dot(table, references, preferred_element_type=jnp.float32)
+    part = jnp.sum(held.astype(jnp.float32) * chosen, axis=1)
+    agreement = lax.psum_scatter(part, "dev", scatter_dimension=0, tiled=True)
     scores = agreement / jnp.sqrt(energy + 1e-06)
     return (wiener(class_sum, weight_sum), scores)
 

time: 315 us -> 201 us (0.64)
  waiting for transfers between devices: 166 us -> 0.01 us
  blocking collectives: 0 us -> 67.3 us
  between operations: 13.9 us -> 1.53 us
  matrix products: 49.2 us -> 38 us
  starting transfers between devices: 0.12 us -> 7.22 us
  local copies, waits for them, and re-layouts: 71.1 us -> 74.3 us
    reduce_scatter x2 -> x0, waiting for transfers between devices: 134 us -> none  [the longest x1 134 us: on_device(): lax.psum_scatter(class_part, 'dev', scatter_dimension=1, tiled=True)]
    unnamed x0 -> x1, blocking collectives: none -> 33.8 us
    all_gather x0 -> x1, blocking collectives: none -> 33.4 us  [on_device(): facts = lax.all_gather(facts, 'dev', axis=1, tiled=True)]
    all_gather x1 -> x0, waiting for transfers between devices: 32.1 us -> none  [on_device(): everything = lax.all_gather(references, 'dev', axis=1, tiled=True)]
    dot_general x2, matrix products: 10.3 us -> 2.86 us  [the longest x1 2.29 us: on_device(): class_sum = jnp.dot(table.T, held, preferred_element_type=jnp.float32)]
    all_to_all x0 -> x1, starting transfers between devices: none -> 7.22 us  [on_device(): lax.all_to_all(aligned, 'dev', split_axis=1, concat_axis=0, tiled=True)]
    unnamed x11 -> x16, local copies, waits for them, and re-layouts: 6.08 us -> 8.22 us
  transfers between devices with their start and end apart: 3 -> 1, of which waited for: 2 -> 0; matrix products, arithmetic and copies ran while one was open for 39% -> 3% of each run, Pallas kernels for 0% -> 0%
where the time goes in v1:
time: 201 us; the launch traced here: 200 us
  local copies, waits for them, and re-layouts  74.3 us (37%)
  blocking collectives  67.3 us (33%)
  matrix products  38 us (19%)
  other arithmetic  11.8 us (6%)
  starting transfers between devices  7.22 us (4%)
    unnamed x1, blocking collectives  33.8 us
    all_gather x1, blocking collectives, on_device(): facts = lax.all_gather(facts, 'dev', axis=1, tiled=True)  33.4 us
    gather x3, local copies, waits for them, and re-layouts, weigh_spectra(): taken = rotations[turn_ids]  17 us
    reshape x1, local copies, waits for them, and re-layouts, transform(): section_z.astype(jnp.bfloat16).reshape(particle_count, BOX, BOX, 2, BAND)  11.4 us
    reshape x1, local copies, waits for them, and re-layouts, transform(): volumes.reshape(-1, BOX)  11.1 us
    convert_element_type x1, local copies, waits for them, and re-layouts, transform(): section_x = jnp.einsum('pxkbz,abxj->pjkaz', section_y, mixing, preferred_...  10.9 us
    dot_general x1, matrix products, weigh_spectra(): jnp.einsum('pmn,pnc->pmc', taken, spectrum, preferred_element_type=jnp.fl...  8.85 us
    dot_general x1, matrix products, transform(): jnp.dot(volumes.reshape(-1, BOX), first_table, preferred_element_type=jnp...  8.38 us
  transfers between devices with their start and end apart: 1, of which 0 were waited for; matrix products, arithmetic and copies ran while one was open for 3% of the time, Pallas kernels for 0%

profile of v1, /device:TPU:0, one launch (start us, length us, event | category | flops | bytes accessed | tf_op | source)
XLA Modules:
  0.0 200.1 jit_solution(11991342504303984840)
XLA Ops:
  0.6 0.0 copy-start
  0.7 0.2 multiply_convert_fusion.2
  0.8 0.2 fusion.65
  1.0 0.1 fusion.55
  1.1 0.1 multiply_convert_fusion.1
  1.3 0.5 fusion.69
  1.8 6.0 %reshape.472 = bf16[2097152]{0:T(1024)(128)(2,1)} reshape(bf16[8,262144]{1,0:T(8,128)(2,1)} %param.7) | data formatting | bytes 8388608
  7.9 11.1 %reshape.440 = bf16[32768,64]{1,0:T(8,128)(2,1)} reshape(bf16[2097152]{0:T(1024)(128)(2,1)} %reshape.472) | data formatting | bytes 8388608 | tf_op jit(solution)/shard_map/reshape | solution.py:31
  18.9 8.4 %fusion = bf16[32768,64]{0,1:T(8,128)(2,1)} fusion(bf16[32768,64]{1,0:T(8,128)(2,1)} %reshape.440, bf16[64,32]{0,1:T(8,128)(2,1)S(1)} %fusion.55, bf16[64,32]{0,1:T(8,128)(2,1)S(1)} %multiply_convert_fusion.1), kind=kOutput, calls=%fused_computation.3 | convolution fusion | flops 270548992 | bytes 8396800 | tf_op jit(solution)/shard_map/dot_general | solution.py:31
  27.3 11.4 %reshape.441 = bf16[8,64,64,2,32]{2,1,0,4,3:T(8,128)(2,1)} reshape(bf16[32768,64]{0,1:T(8,128)(2,1)} %fusion) | data formatting | bytes 8388608 | tf_op jit(solution)/shard_map/reshape | solution.py:32
  38.7 7.5 %fusion.8 = bf16[8,64,32,2,32]{1,2,4,0,3:T(8,128)(2,1)S(1)} fusion(bf16[8,64,64,2,32]{2,1,0,4,3:T(8,128)(2,1)} %reshape.441, bf16[1,2,64,32]{2,3,1,0:T(8,128)(2,1)S(1)} %get-tuple-element.15, bf16[1,2,64,32]{2,3,1,0:T(8,128)(2,1)S(1)} %get-tuple-element.14), kind=kOutput, calls=%fused_computation.14 | convolution fusion | flops 269516800 | bytes 6307840 | tf_op jit(solution)/shard_map/pxybz,abyj->pxjaz/dot_general | solution.py:33
  46.2 5.5 %fusion.9 = bf16[8,32,32,2,32]{4,1,2,0,3:T(8,128)(2,1)} fusion(bf16[8,64,32,2,32]{1,2,4,0,3:T(8,128)(2,1)S(1)} %fusion.8, bf16[1,2,64,32]{2,3,1,0:T(8,128)(2,1)S(1)} %get-tuple-element.15, bf16[1,2,64,32]{2,3,1,0:T(8,128)(2,1)S(1)} %get-tuple-element.14), kind=kOutput, calls=%fused_computation.15 | convolution fusion | flops 134774784 | bytes 3162112 | tf_op jit(solution)/shard_map/pxkbz,abxj->pjkaz/dot_general | solution.py:36
  51.6 10.9 %copy.30 = bf16[8,32,32,2,32]{2,1,4,3,0:T(8,128)(2,1)} copy(bf16[8,32,32,2,32]{4,1,2,0,3:T(8,128)(2,1)} %fusion.9) | data formatting | bytes 2097152 | tf_op jit(solution)/shard_map/convert_element_type | solution.py:38
  62.5 7.0 %reshape.442 = bf16[8,1024,64]{1,2,0:T(8,128)(2,1)} reshape(bf16[8,32,32,2,32]{2,1,4,3,0:T(8,128)(2,1)} %copy.30) | data formatting | bytes 2097152 | tf_op jit(solution)/shard_map/reshape | solution.py:39
  69.5 5.6 %fusion.76 = (bf16[3,512,1024]{2,1,0:T(8,128)(2,1)}, bf16[3,512,1024]{2,1,0:T(8,128)(2,1)S(1)}) fusion(bf16[3,1024,1024]{2,1,0:T(8,128)(2,1)} %param.8), kind=kLoop, calls=%fused_computation.127 | loop fusion | bytes 12582912 | tf_op jit(solution)/shard_map/gather | solution.py:57
  75.1 0.0 copy-done.3
  75.2 0.6 pad_clamp_fusion
  75.8 6.6 %gather_fusion = bf16[8,512,1024]{2,1,0:T(8,128)(2,1)} fusion(bf16[3,512,1024]{2,1,0:T(8,128)(2,1)} %get-tuple-element.10, s32[1024]{0:T(1024)} %pad_clamp_fusion), kind=kCustom, calls=%fused_computation | custom fusion | bytes 16777248 | tf_op jit(solution)/shard_map/gather | solution.py:57
  82.4 4.7 %gather_fusion.1 = bf16[8,512,1024]{2,1,0:T(8,128)(2,1)} fusion(bf16[3,512,1024]{2,1,0:T(8,128)(2,1)S(1)} %get-tuple-element.11, s32[1024]{0:T(1024)} %pad_clamp_fusion), kind=kCustom, calls=%fused_computation.1 | custom fusion | bytes 16777248 | tf_op jit(solution)/shard_map/gather | solution.py:57
  87.1 0.8 slice_bitcast_fusion.3
  87.9 0.1 broadcast_multiply_fusion
  88.0 0.7 add_convert_fusion
  88.7 0.0 copy-start.2
  88.7 8.9 %fusion.1 = f32[8,1024,64]{1,2,0:T(8,128)S(1)} fusion(bf16[8,1024,64]{1,2,0:T(8,128)(2,1)} %reshape.442, bf16[8,512,1024]{2,1,0:T(8,128)(2,1)} %gather_fusion.1, bf16[8,512,1024]{2,1,0:T(8,128)(2,1)} %gather_fusion), kind=kOutput, calls=%fused_computation.4 | convolution fusion | flops 1107296256 | bytes 19922944 | tf_op jit(solution)/shard_map/pmn,pnc->pmc/dot_general | solution.py:58
  97.6 0.1 multiply_add_fusion
  97.7 0.0 copy-done.2
  97.7 8.2 %subtract_multiply_fusion = (bf16[8,1024,32]{1,2,0:T(8,128)(2,1)S(1)}, bf16[8,1024,32]{1,2,0:T(8,128)(2,1)S(1)}) fusion(f32[8,1024,64]{1,2,0:T(8,128)S(1)} %fusion.1, s32[8,32]{1,0:T(8,128)S(1)} %broadcast_multiply_fusion, s32[8,1024]{1,0:T(8,128)S(1)} %multiply_add_fusion, f32[1024,32]{0,1:T(8,128)S(1)} %add_convert_fusion, f32[8]{0:T(128)S(1)} %copy-done.2), kind=kLoop, calls=%fused_computation.39 | loop fusion | flops 7077888 | bytes 3310624 | tf_op jit(solution)/shard_map/mul | solution.py:73
  105.9 0.3 multiply_reduce_fusion
  106.2 1.1 copy.31
  107.3 0.0 copy-start.1
  107.3 1.7 convert_element_type.133
  109.0 0.0 copy-start.4
  109.0 0.0 copy-start.5
  109.0 1.5 copy.32
  110.6 7.2 %all-to-all-start = ((bf16[8,16,4096]{2,0,1:T(8,128)(2,1)}), bf16[8,16,4096]{2,0,1:T(8,128)(2,1)S(1)}, u32[]{:S(2)}, u32[]{:S(2)}) async-start(bf16[8,16,4096]{2,0,1:T(8,128)(2,1)} %copy.32), calls=%async_computation | async-start | bytes 2097152 | tf_op jit(solution)/shard_map/all_to_all | solution.py:99
  117.8 33.4 %all-gather = f32[16,8,2]{1,2,0:T(2,128)S(1)} all-gather(f32[1,8,2]{1,2,0:T(2,128)S(1)} %maximum_bitcast_fusion.5), channel_id=1, replica_groups=mesh['groups'=2,'dev'=16] {'dev'}, dimensions={0}, use_global_device_ids=true | all-gather | bytes 1088 | tf_op jit(solution)/shard_map/all_gather | solution.py:98
  151.3 0.1 reshape.463
  151.4 0.6 dynamic-slice
  152.7 0.1 add_convert_fusion.1
  152.7 4.9 %convolution_add_fusion = f32[48,64,32]{1,0,2:T(8,128)S(1)} fusion(f32[64,32]{0,1:T(8,128)S(1)} %add_convert_fusion.1, f32[128]{0:T(128)S(1)} %get-tuple-element.20, f32[128]{0:T(128)S(1)} %get-tuple-element.19), kind=kOutput, calls=%fused_computation.28 | convolution fusion | flops 152147968 | bytes 402432 | tf_op jit(solution)/shard_map/dot_general | solution.py:106
  157.7 0.0 all-to-all-done
  157.7 0.6 fusion.17
  158.3 33.8 %all-reduce = f32[128]{0:T(128)S(1)} all-reduce(f32[128]{0:T(128)S(1)} %fusion.17), channel_id=2, replica_groups=mesh['groups'=2,'dev'=16] {'dev'}, use_global_device_ids=true, to_apply=%region_1.2.clone | all-reduce | flops 128 | bytes 1024
  192.1 0.7 copy.33
  192.8 2.3 %convolution_divide_fusion = f32[48,64,2,32]{1,0,3,2:T(8,128)} fusion(bf16[64,2,32,128]{3,2,1,0:T(8,128)(2,1)S(1)} %bitcast.84, f32[48,64,32]{1,0,2:T(8,128)S(1)} %convolution_add_fusion, f32[128]{0:T(128)S(1)} %get-tuple-element.19), kind=kOutput, calls=%fused_computation.26 | convolution fusion | flops 50534400 | bytes 2228736 | tf_op jit(solution)/shard_map/dot_general | solution.py:105
  195.1 3.0 %copy.35 = f32[48,64,2,32]{0,3,2,1:T(8,128)S(1)} copy(f32[48,64,2,32]{1,0,3,2:T(8,128)} %convolution_divide_fusion) | data formatting | bytes 1572864 | tf_op jit(solution)/shard_map/div | solution.py:84
  198.1 1.5 copy.36
  199.5 0.6 dynamic-slice_multiply_fusion
  (15 shorter events, 0.1 us)
Async XLA Ops:
  0.6 157.1 %copy-start = (bf16[48,4096]{1,0:T(8,128)(2,1)S(1)}, bf16[48,4096]{1,0:T(8,128)(2,1)}, u32[]{:S(2)}) copy-start(bf16[48,4096]{1,0:T(8,128)(2,1)} %param.13) | copy-start | bytes 1179652
  69.5 5.7 %copy-start.3 = (s32[8]{0:T(128)S(1)}, s32[8]{0:T(128)}, u32[]{:S(2)}) copy-start(s32[8]{0:T(128)} %param.9) | copy-start | bytes 100
  88.7 9.0 %copy-start.2 = (f32[8]{0:T(128)S(1)}, f32[8]{0:T(128)}, u32[]{:S(2)}) copy-start(f32[8]{0:T(128)} %param.11) | copy-start | bytes 100
  107.3 45.4 %copy-start.1 = (s32[32]{0:T(128)S(1)}, s32[32]{0:T(128)}, u32[]{:S(2)}) copy-start(s32[32]{0:T(128)} %fusion.69) | copy-start | bytes 388
  109.0 8.8 %copy-start.4 = (s32[8]{0:T(128)S(1)}, s32[8]{0:T(128)}, u32[]{:S(2)}) copy-start(s32[8]{0:T(128)} %param.12) | copy-start | bytes 100
  109.0 42.4 %copy-start.5 = (u32[32]{0:T(128)S(1)}, u32[32]{0:T(128)}, u32[]{:S(2)}) copy-start(u32[32]{0:T(128)} %constant.119) | copy-start | bytes 388
  110.6 47.1 %all-to-all-start = ((bf16[8,16,4096]{2,0,1:T(8,128)(2,1)}), bf16[8,16,4096]{2,0,1:T(8,128)(2,1)S(1)}, u32[]{:S(2)}, u32[]{:S(2)}) async-start(bf16[8,16,4096]{2,0,1:T(8,128)(2,1)} %copy.32), calls=%async_computation | async-start | bytes 2097152 | tf_op jit(solution)/shard_map/all_to_all | solution.py:99

commit v2 on v0

v2 whole, which is shorter than its diff:
```python
import math

import jax
import jax.numpy as jnp
import ml_dtypes
import numpy as np
from jax import lax
from jax.experimental import pallas as pl
from jax.experimental.pallas import tpu as pltpu
from jax.sharding import PartitionSpec as P

BOX = 64
BAND = 32
ROWS = 8
CELLS = BAND * BAND
LANES = 128
TWO_PI = 2.0 * math.pi
VMEM = pl.BlockSpec(memory_space=pltpu.VMEM)
SMEM = pl.BlockSpec(memory_space=pltpu.SMEM)
F32 = jnp.float32
BF16 = jnp.bfloat16


def rounded(table):
    return np.asarray(table, np.float32).astype(ml_dtypes.bfloat16)


def tables():
    n = np.arange(BOX)
    k = np.arange(BAND) - BAND // 2
    angle = TWO_PI * ((n[:, None] * k[None, :]) % BOX) / BOX
    cosine, sine = np.cos(angle) / 8.0, np.sin(angle) / 8.0
    by_z = np.zeros((4, 64, 2, 4, 32))
    for y in range(4):
        by_z[y, :, 0, y] = cosine
        by_z[y, :, 1, y] = -sine
    mixing = np.array([[cosine, sine], [-sine, cosine]])
    by_x = np.zeros((8, 2, 2, 16, 2, 64, 8))
    for p in range(8):
        by_x[p, :, :, :, :, :, p] = mixing.reshape(2, 2, 64, 2, 16).transpose(3, 0, 4, 1, 2)
    q = np.arange(16)
    turn = TWO_PI * ((q[:, None] * q[None, :]) % 16) / 16
    c, s = np.cos(turn) / 4.0, np.sin(turn) / 4.0
    by_h = np.zeros((16, 2, 16, 16, 2, 16))
    for low in range(16):
        by_h[:, 0, low, :, 0, low] = c
        by_h[:, 0, low, :, 1, low] = s
        by_h[:, 1, low, :, 0, low] = -s
        by_h[:, 1, low, :, 1, low] = c
    by_y = np.zeros((16, 2, 4, 32, 2, 2, 2, 32))
    for high in range(2):
        for y in range(4):
            part = TWO_PI * (((high * 16 + q - 16) * y) % 64) / 64
            c, s = (np.cos(part) / 2.0)[:, None], (np.sin(part) / 2.0)[:, None]
            z = np.arange(32)
            by_y[:, 0, y, z, high, 0, 0, z] = c
            by_y[:, 1, y, z, high, 0, 0, z] = s
            by_y[:, 0, y, z, high, 0, 1, z] = -s
            by_y[:, 1, y, z, high, 0, 1, z] = c
            by_y[:, 0, y, z, high, 1, 0, z] = s
            by_y[:, 1, y, z, high, 1, 0, z] = -c
            by_y[:, 0, y, z, high, 1, 1, z] = c
            by_y[:, 1, y, z, high, 1, 1, z] = s
    return (
        rounded(by_z.reshape(256, 256)),
        rounded(by_x.reshape(512, 1024)),
        rounded(by_h.reshape(512, 512)),
        rounded(by_y.reshape(16, 256, 256)),
    )


def dot(a, b):
    return jnp.dot(a, b, preferred_element_type=F32)


def root(count):
    angle = (count - 64.0 * jnp.floor(count / 64.0)) * (TWO_PI / 64.0)
    return jnp.cos(angle), jnp.sin(angle)


def halves(x):
    high = x.astype(BF16).astype(F32)
    return high, x - high


def factors(facts):
    defocus, sx, sy, sz = (facts[:, i : i + 1] for i in range(1, 5))
    cell = lax.broadcasted_iota(jnp.int32, (ROWS, CELLS), 1)
    kx = (cell // BAND - BAND // 2).astype(F32)
    ky = (cell % BAND - BAND // 2).astype(F32)
    focus = defocus * (kx * kx + ky * ky) / BAND + 0.3
    cos_a, sin_a = root(kx * sx + ky * sy)
    cos_f, sin_f = jnp.cos(focus), jnp.sin(focus)
    rows = [halves(x) for x in (sin_f * cos_a, sin_f * sin_a, cos_f * cos_a, cos_f * sin_a)]
    lane = lax.broadcasted_iota(jnp.int32, (ROWS, LANES), 1)
    kz = (lane % BAND - BAND // 2).astype(F32)
    cos_b, sin_b = root(kz * sz)
    first = lane < LANES // 2
    one = jnp.where(first, cos_b, sin_b)
    two = jnp.where(first, -sin_b, cos_b)
    focus = defocus * (kz * kz) / BAND
    cos_f, sin_f = jnp.cos(focus), jnp.sin(focus)
    lanes = [halves(x) for x in (cos_f * one, cos_f * two, sin_f * one, sin_f * two)]
    blank = jnp.zeros((32, CELLS), F32)
    left = jnp.concatenate(
        [r[0] for r in rows] + [r[0] for r in rows] + [r[1] for r in rows] + [blank], axis=0
    )
    right = jnp.concatenate(
        [x[0] for x in lanes] + [x[1] for x in lanes] + [x[0] for x in lanes] + [blank[:, :LANES]], axis=0
    )
    owner = lax.broadcasted_iota(jnp.int32, (LANES, LANES), 0) % ROWS
    right = [jnp.where(owner == p, right, 0.0) for p in range(ROWS)]
    return left.T.astype(BF16), jnp.concatenate(right, axis=1).astype(BF16)


def spectra(turn_ref, vol_ref, rot_ref, facts_ref, z_ref, x_ref, h_ref, y_ref,
            out_ref, energy_ref, by_z, by_x, by_h, spec, left_ref, right_ref, wide):
    owners, _, pairs, _ = out_ref.shape
    left, right = factors(facts_ref[...])
    left_ref[...] = left
    right_ref[...] = right

    @pl.loop(0, 16)
    def _(h):
        got = dot(vol_ref[:, pl.ds(pl.multiple_of(h * 256, 256), 256)], z_ref[...]).astype(BF16)
        at = pl.ds(pl.multiple_of(h * 128, 128), 128)
        by_z[0:512, at] = got[:, :128]
        by_z[512:1024, at] = got[:, 128:]

    @pl.loop(0, 8)
    def _(h2):
        got = dot(x_ref[...], by_z[:, pl.ds(pl.multiple_of(h2 * 256, 256), 256)]).astype(BF16)
        for i in range(2):
            to = pl.ds(pl.multiple_of(h2 * 64 + i * 32, 32), 32)
            for g in range(16):
                by_x[to, g * 128 : (g + 1) * 128] = got[g * 32 : (g + 1) * 32, i * 128 : (i + 1) * 128]

    @pl.loop(0, 8)
    def _(g2):
        got = dot(h_ref[...], by_x[:, pl.ds(pl.multiple_of(g2 * 256, 256), 256)]).astype(BF16)
        got = got.reshape(16, 2, 16, 256)
        for i in range(2):
            to = pl.ds(pl.multiple_of(g2 * 32 + i * 16, 16), 16)
            for c in range(2):
                by_h[:, to, c * 128 : (c + 1) * 128] = got[:, c, :, i * 128 : (i + 1) * 128]

    @pl.loop(0, 16)
    def _(q):
        got = dot(by_h[q], y_ref[q])
        for high in range(2):
            spec[pl.ds(high * 16 + q, 256, stride=32), :] = got[:, high * 128 : (high + 1) * 128]

    first = lax.broadcasted_iota(jnp.int32, (CELLS // 2, LANES), 1) < LANES // 2

    @pl.loop(0, ROWS)
    def _(p):
        own = spec[pl.ds(pl.multiple_of(p * CELLS, CELLS), CELLS), :].astype(BF16)
        turned = dot(rot_ref[turn_ref[p]], own)
        factor = dot(left_ref[...], right_ref[:, pl.ds(pl.multiple_of(p * 128, 128), 128)])
        both = turned * factor
        wide[...] = both + pltpu.roll(both, LANES // 2, 1)
        packed = jnp.where(first, wide[pl.ds(0, CELLS // 2, stride=2), :], wide[pl.ds(1, CELLS // 2, stride=2), :])
        packed = packed.astype(BF16)
        out_ref[:, p] = packed.reshape(owners, pairs, LANES)
        long = packed.astype(F32)
        energy_ref[pl.ds(p, 1), :] = jnp.sum(long * long, axis=0, keepdims=True)


def classes(owners, send_ref, facts_ref, energy_ref, refs_ref, new_ref, score_ref,
            held, facts, wide, chosen, below, parts, answer, sems):
    me = lax.axis_index("dev")
    class_count, columns = refs_ref.shape
    pairs = columns // LANES
    particles = owners * ROWS

    def copy(i, k):
        to = lax.rem(me + k, owners)
        src = (facts_ref, send_ref.at[to], parts.at[to])[i]
        dst = (facts, held, answer)[i]
        return pltpu.make_async_remote_copy(
            src_ref=src, dst_ref=dst.at[me],
            send_sem=sems.at[2 * i, k], recv_sem=sems.at[2 * i + 1, k],
            device_id={"dev": to}, device_id_type=pl.DeviceIdType.MESH,
        )

    barrier = pltpu.get_barrier_semaphore()

    @pl.loop(1, owners)
    def _(k):
        pl.semaphore_signal(
            barrier, inc=1, device_id={"dev": lax.rem(me + k, owners)}, device_id_type=pl.DeviceIdType.MESH
        )

    pl.semaphore_wait(barrier, owners - 1)

    @pl.loop(1, owners)
    def _(k):
        copy(0, k).start()

    @pl.loop(1, owners)
    def _(k):
        copy(1, k).start()

    facts[me] = facts_ref[...]
    held[me] = send_ref[me]

    @pl.loop(1, owners)
    def _(k):
        copy(0, k).wait()

    known = facts[...].reshape(particles, LANES)
    lane = lax.broadcasted_iota(jnp.int32, (particles, LANES), 1)
    member = jnp.where(known[:, 0:1] == lane.astype(F32), 1.0, 0.0)
    across = member.T[:class_count]
    defocus = known[:, 1:2]
    one = lax.broadcasted_iota(jnp.int32, (1, LANES), 1)
    kz = one % BAND - BAND // 2

    @pl.loop(0, pairs)
    def _(r):
        cell = (me * pairs + r) * 2 + one // (2 * BAND)
        kx = cell // BAND - BAND // 2
        ky = cell % BAND - BAND // 2
        radius = (kx * kx + ky * ky + kz * kz).astype(F32)
        weight = jnp.sin(defocus * radius / BAND + 0.3)
        total = jnp.dot(across, weight * weight, preferred_element_type=F32, precision=lax.Precision.HIGHEST)
        below[r] = 1.0 / (total + 1.0)
        at = pl.ds(pl.multiple_of(r * LANES, LANES), LANES)
        chosen[r] = dot(member[:, :class_count].astype(BF16), refs_ref[:, at])

    @pl.loop(1, owners)
    def _(k):
        copy(1, k).wait()

    wide[...] = held[...].astype(F32).reshape(particles * pairs, LANES)
    parts[...] = jnp.zeros_like(parts)

    @pl.loop(0, pairs)
    def _(r):
        rows = wide[pl.ds(r, particles, stride=pairs), :]
        total = dot(across.astype(BF16), rows.astype(BF16))
        new_ref[:, pl.ds(pl.multiple_of(r * LANES, LANES), LANES)] = total * below[r]
        parts[...] += (rows * chosen[r]).reshape(owners, ROWS, LANES)

    @pl.loop(1, owners)
    def _(k):
        copy(2, k).start()

    answer[me] = parts[me]

    @pl.loop(1, owners)
    def _(k):
        copy(2, k).wait()

    agreement = jnp.sum(jnp.sum(answer[...], axis=0), axis=1, keepdims=True)
    energy = jnp.sum(energy_ref[...], axis=1, keepdims=True)
    score_ref[...] = jnp.broadcast_to(agreement / jnp.sqrt(energy + 1e-06), (ROWS, LANES))


def on_device(owners, volumes, rotations, turn_ids, shifts, defocus, labels, references):
    class_count, columns = references.shape
    pairs = columns // LANES
    particles = owners * ROWS
    facts = jnp.concatenate(
        [labels.astype(F32)[:, None], defocus[:, None], shifts.astype(F32), jnp.zeros((ROWS, LANES - 5), F32)], axis=1
    )
    rows = volumes.reshape(ROWS, BOX, BOX * BOX).transpose(1, 0, 2).reshape(BOX * ROWS, BOX * BOX)
    send, energy = pl.pallas_call(
        spectra,
        out_shape=(
            jax.ShapeDtypeStruct((owners, ROWS, pairs, LANES), BF16),
            jax.ShapeDtypeStruct((ROWS, LANES), F32),
        ),
        in_specs=[SMEM] + [VMEM] * 7,
        out_specs=(VMEM, VMEM),
        scratch_shapes=[
            pltpu.VMEM((1024, 2048), BF16),
            pltpu.VMEM((512, 2048), BF16),
            pltpu.VMEM((16, 256, 256), BF16),
            pltpu.VMEM((ROWS * CELLS, LANES), F32),
            pltpu.VMEM((CELLS, LANES), BF16),
            pltpu.VMEM((LANES, ROWS * LANES), BF16),
            pltpu.VMEM((CELLS, LANES), F32),
        ],
        compiler_params=pltpu.CompilerParams(vmem_limit_bytes=48 * 1024 * 1024),
    )(turn_ids, rows, rotations, facts, *(jnp.asarray(t) for t in tables()))
    new_refs, scores = pl.pallas_call(
        lambda *refs: classes(owners, *refs),
        out_shape=(
            jax.ShapeDtypeStruct((class_count, columns), F32),
            jax.ShapeDtypeStruct((ROWS, LANES), F32),
        ),
        in_specs=[VMEM] * 4,
        out_specs=(VMEM, VMEM),
        scratch_shapes=[
            pltpu.VMEM((owners, ROWS, pairs, LANES), BF16),
            pltpu.VMEM((owners, ROWS, LANES), F32),
            pltpu.VMEM((particles * pairs, LANES), F32),
            pltpu.VMEM((pairs, particles, LANES), F32),
            pltpu.VMEM((pairs, class_count, LANES), F32),
            pltpu.VMEM((owners, ROWS, LANES), F32),
            pltpu.VMEM((owners, ROWS, LANES), F32),
            pltpu.SemaphoreType.DMA((6, owners)),
        ],
        compiler_params=pltpu.CompilerParams(
            collective_id=0, has_side_effects=True, vmem_limit_bytes=48 * 1024 * 1024
        ),
    )(send, facts, energy, references)
    return new_refs, scores[:, 0]


def solution(mesh):
    owners = mesh.shape["dev"]
    return jax.shard_map(
        lambda *args: on_device(owners, *args),
        mesh=mesh,
        in_specs=(
            P(("groups", "dev"), None),
            P(),
            P(("groups", "dev")),
            P(("groups", "dev"), None),
            P(("groups", "dev")),
            P(("groups", "dev")),
            P("groups", "dev"),
        ),
        out_specs=(P("groups", "dev"), P(("groups", "dev"))),
        check_vma=False,
    )
```

time: 315 us -> 85.3 us (0.27)
  waiting for transfers between devices: 166 us -> 0 us
  Pallas kernels: 0 us -> 75 us
  local copies, waits for them, and re-layouts: 71.1 us -> 8.57 us
  matrix products: 49.2 us -> 0 us
  between operations: 13.9 us -> 0.66 us
  other arithmetic: 13.1 us -> 0.74 us
    reduce_scatter x2 -> x0, waiting for transfers between devices: 134 us -> none  [the longest x1 134 us: on_device(): lax.psum_scatter(class_part, 'dev', scatter_dimension=1, tiled=True)]
    pallas_call x0 -> x2, Pallas kernels: none -> 75 us  [the longest x1 47 us: on_device(): pl.pallas_call(lambda *refs: classes(owners, *refs), out_shape=(jax.Shape...]
    dot_general x7 -> x0, matrix products: 49.2 us -> none  [the longest x1 9 us: transform(): jnp.dot(volumes.reshape(-1, BOX), first_table, preferred_element_type=jnp...]
    all_gather x1 -> x0, waiting for transfers between devices: 32.1 us -> none  [on_device(): everything = lax.all_gather(references, 'dev', axis=1, tiled=True)]
    reshape x3 -> x0, local copies, waits for them, and re-layouts: 29.8 us -> none  [the longest x1 11.5 us: transform(): section_z.astype(jnp.bfloat16).reshape(particle_count, BOX, BOX, 2, BAND)]
    gather x3 -> x0, local copies, waits for them, and re-layouts: 16.9 us -> none  [weigh_spectra(): taken = rotations[turn_ids]]
    convert_element_type x3 -> x0, local copies, waits for them, and re-layouts: 13.5 us -> none  [the longest x1 10.9 us: transform(): section_x = jnp.einsum('pxkbz,abxj->pjkaz', section_y, mixing, preferred_...]
    mul x3 -> x0, other arithmetic: 8.29 us -> none  [the longest x1 8.21 us: weigh_spectra(): weight * (real_part * cosine - imag_part * sine_part)]
  transfers between devices with their start and end apart: 3 -> 0, of which waited for: 2 -> 0; matrix products, arithmetic and copies ran while one was open for 39% -> 0% of each run, Pallas kernels for 0% -> 0%
where the time goes in v2:
time: 85.3 us; the launch traced here: 85 us
  Pallas kernels  75 us (88%)
  local copies, waits for them, and re-layouts  8.57 us (10%)
    pallas_call x1, Pallas kernels, on_device(): pl.pallas_call(lambda *refs: classes(owners, *refs), out_shape=(jax.Shape...  47 us
    pallas_call x1, Pallas kernels, on_device(): pl.pallas_call(spectra, out_shape=(jax.ShapeDtypeStruct((owners, ROWS, pa...  28 us
    unnamed x14, local copies, waits for them, and re-layouts  7.05 us

profile of v2, /device:TPU:0, one launch (start us, length us, event | category | flops | bytes accessed | tf_op | source)
XLA Modules:
  0.0 85.0 jit_solution(5513397917406143339)
XLA Ops:
  0.6 0.7 convert_bitcast_fusion
  1.3 0.1 pad.3.clone
  1.4 0.1 copy.17
  1.4 0.8 copy.16
  2.2 0.7 copy.18
  2.9 0.1 maximum_maximum_fusion.facts_ref.refs_1_
  3.0 0.0 copy-start
  3.0 1.6 %copy-done = bf16[16,256,256]{2,1,0:T(8,128)(2,1)S(1)} copy-done((bf16[16,256,256]{2,1,0:T(8,128)(2,1)S(1)}, bf16[16,256,256]{2,1,0:T(8,128)(2,1)}, u32[]{:S(2)}) %copy-start) | copy-done | bytes 2097176
  4.6 0.0 copy-start.1
  4.6 1.2 %copy-done.1 = bf16[512,1024]{1,0:T(8,128)(2,1)S(1)} copy-done((bf16[512,1024]{1,0:T(8,128)(2,1)S(1)}, bf16[512,1024]{1,0:T(8,128)(2,1)}, u32[]{:S(2)}) %copy-start.1) | copy-done | bytes 1048600
  5.8 0.0 copy-start.2
  5.8 1.0 %copy-done.2 = bf16[512,512]{1,0:T(8,128)(2,1)S(1)} copy-done((bf16[512,512]{1,0:T(8,128)(2,1)S(1)}, bf16[512,512]{1,0:T(8,128)(2,1)}, u32[]{:S(2)}) %copy-start.2) | copy-done | bytes 524312
  6.9 0.0 copy-start.4
  6.9 0.9 %copy-done.4 = bf16[256,256]{1,0:T(8,128)(2,1)S(1)} copy-done((bf16[256,256]{1,0:T(8,128)(2,1)S(1)}, bf16[256,256]{1,0:T(8,128)(2,1)}, u32[]{:S(2)}) %copy-start.4) | copy-done | bytes 131096
  7.8 0.0 copy-start.5
  7.8 0.7 copy-done.5
  8.4 0.0 copy-start.3
  8.4 28.0 %shard_map.122 = (bf16[16,8,32,128]{3,2,1,0:T(8,128)(2,1)S(1)}, f32[8,128]{1,0:T(8,128)S(1)}) custom-call(s32[8]{0:T(128)S(1)} %copy-done.5, bf16[512,4096]{1,0:T(8,128)(2,1)} %bitcast.8, bf16[3,1024,1024]{2,1,0:T(8,128)(2,1)} %rot_ref.1, f32[8,128]{1,0:T(8,128)S(1)} %maximum_maximum_fusion.facts_ref.refs_1_, bf16[256,256]{1,0:T(8,128)(2,1)S(1)} %copy-done.4, ...), custom_call_target="tpu_custom_call" | custom-call | tf_op jit(solution)/shard_map/pallas_call | solution.py:268
  36.4 0.0 copy-done.3
  36.5 47.0 %shard_map.123 = (f32[48,4096]{1,0:T(8,128)S(1)}, f32[8,128]{1,0:T(8,128)S(1)}) custom-call(bf16[16,8,32,128]{3,2,1,0:T(8,128)(2,1)S(1)} %get-tuple-element.6.refs_0_, f32[8,128]{1,0:T(8,128)S(1)} %maximum_maximum_fusion.facts_ref.refs_1_, f32[8,128]{1,0:T(8,128)S(1)} %get-tuple-element.7.refs_2_, bf16[48,4096]{1,0:T(8,128)(2,1)S(1)} %copy-done.3), custom_call_target="tpu_custom_call" | custom-call | tf_op jit(solution)/shard_map/pallas_call | solution.py:287
  83.5 0.6 slice_reduce_fusion
  84.1 0.9 %copy.20 = f32[48,4096]{1,0:T(8,128)} copy(f32[48,4096]{1,0:T(8,128)S(1)} %get-tuple-element.12) | data formatting | bytes 1572864
  (2 shorter events, 0.0 us)
Async XLA Ops:
  3.0 1.6 %copy-start = (bf16[16,256,256]{2,1,0:T(8,128)(2,1)S(1)}, bf16[16,256,256]{2,1,0:T(8,128)(2,1)}, u32[]{:S(2)}) copy-start(bf16[16,256,256]{2,1,0:T(8,128)(2,1)} %constant.13.clone.y_ref) | copy-start | bytes 6291460
  4.6 1.2 %copy-start.1 = (bf16[512,1024]{1,0:T(8,128)(2,1)S(1)}, bf16[512,1024]{1,0:T(8,128)(2,1)}, u32[]{:S(2)}) copy-start(bf16[512,1024]{1,0:T(8,128)(2,1)} %constant.11.clone.x_ref) | copy-start | bytes 3145732
  5.8 1.0 %copy-start.2 = (bf16[512,512]{1,0:T(8,128)(2,1)S(1)}, bf16[512,512]{1,0:T(8,128)(2,1)}, u32[]{:S(2)}) copy-start(bf16[512,512]{1,0:T(8,128)(2,1)} %constant.12.clone.h_ref) | copy-start | bytes 1572868
  6.9 0.9 %copy-start.4 = (bf16[256,256]{1,0:T(8,128)(2,1)S(1)}, bf16[256,256]{1,0:T(8,128)(2,1)}, u32[]{:S(2)}) copy-start(bf16[256,256]{1,0:T(8,128)(2,1)} %constant.10.clone.z_ref) | copy-start | bytes 393220
  7.8 0.7 copy-start.5
  8.4 28.0 %copy-start.3 = (bf16[48,4096]{1,0:T(8,128)(2,1)S(1)}, bf16[48,4096]{1,0:T(8,128)(2,1)}, u32[]{:S(2)}) copy-start(bf16[48,4096]{1,0:T(8,128)(2,1)} %refs_3_.1) | copy-start | bytes 1179652

commit v3 on v2

--- a/solution.py
+++ b/solution.py
@@ -14,8 +14,11 @@
 ROWS = 8
 CELLS = BAND * BAND
 LANES = 128
+CHUNKS = 4
+GROUP = 2
 TWO_PI = 2.0 * math.pi
 VMEM = pl.BlockSpec(memory_space=pltpu.VMEM)
+HBM = pl.BlockSpec(memory_space=pltpu.HBM)
 SMEM = pl.BlockSpec(memory_space=pltpu.SMEM)
 F32 = jnp.float32
 BF16 = jnp.bfloat16
@@ -113,19 +116,84 @@
     return left.T.astype(BF16), jnp.concatenate(right, axis=1).astype(BF16)
 
 
-def spectra(turn_ref, vol_ref, rot_ref, facts_ref, z_ref, x_ref, h_ref, y_ref,
-            out_ref, energy_ref, by_z, by_x, by_h, spec, left_ref, right_ref, wide):
-    owners, _, pairs, _ = out_ref.shape
-    left, right = factors(facts_ref[...])
+def collect(labels, defocus, shifts):
+    row = lax.broadcasted_iota(jnp.int32, (ROWS, LANES), 0)
+    lane = lax.broadcasted_iota(jnp.int32, (ROWS, LANES), 1)
+    facts = jnp.zeros((ROWS, LANES), F32)
+    for p in range(ROWS):
+        values = [labels[p].astype(F32), defocus[p]] + [shifts[i, p].astype(F32) for i in range(3)]
+        for i, value in enumerate(values):
+            facts = jnp.where((row == p) & (lane == i), value, facts)
+    return facts
+
+
+def whole(owners, turn_ref, label_ref, defocus_ref, shift_ref, vol_hbm, rot_hbm, refs_hbm,
+          z_hbm, x_hbm, h_hbm, y_hbm, new_ref, score_ref,
+          vol_ref, rot_ref, refs_ref, z_ref, x_ref, h_ref, y_ref,
+          by_z, by_x, by_h, spec, left_ref, right_ref, wide, energy_ref,
+          send, held, facts_ref, facts, chosen, below, parts, answer, load_sems, fact_sems, data_sems, answer_sems):
+    me = lax.axis_index("dev")
+    class_count, columns = refs_ref.shape
+    pairs = columns // LANES
+    particles = owners * ROWS
+
+    def load(i):
+        if i < CHUNKS:
+            at = pl.ds(i * (4096 // CHUNKS), 4096 // CHUNKS)
+            src, dst = vol_hbm.at[:, at], vol_ref.at[:, at]
+        else:
+            src, dst = (
+                (z_hbm, z_ref), (x_hbm, x_ref), (h_hbm, h_ref), (y_hbm, y_ref), (rot_hbm, rot_ref), (refs_hbm, refs_ref)
+            )[i - CHUNKS]
+        return pltpu.make_async_copy(src, dst, load_sems.at[i])
+
+    for i in (CHUNKS, *range(CHUNKS), *range(CHUNKS + 1, CHUNKS + 6)):
+        load(i).start()
+
+    def remote(src, dst, sems, to, k):
+        return pltpu.make_async_remote_copy(
+            src_ref=src, dst_ref=dst, send_sem=sems.at[0, k], recv_sem=sems.at[1, k],
+            device_id={"dev": to}, device_id_type=pl.DeviceIdType.MESH,
+        )
+
+    def fact_copy(k):
+        return remote(facts_ref, facts.at[me], fact_sems, lax.rem(me + k, owners), k)
+
+    def data_copy(g, k):
+        to = lax.rem(me + k, owners)
+        at = pl.ds(g * GROUP, GROUP)
+        return remote(send.at[to, at], held.at[me, at], data_sems.at[g], to, k)
+
+    def answer_copy(k):
+        to = lax.rem(me + k, owners)
+        return remote(parts.at[to], answer.at[me], answer_sems, to, k)
+
+    barrier = pltpu.get_barrier_semaphore()
+
+    @pl.loop(1, owners)
+    def _(k):
+        pl.semaphore_signal(
+            barrier, inc=1, device_id={"dev": lax.rem(me + k, owners)}, device_id_type=pl.DeviceIdType.MESH
+        )
+
+    own_facts = collect(label_ref, defocus_ref, shift_ref)
+    facts_ref[...] = own_facts
+    left, right = factors(own_facts)
     left_ref[...] = left
     right_ref[...] = right
 
-    @pl.loop(0, 16)
-    def _(h):
-        got = dot(vol_ref[:, pl.ds(pl.multiple_of(h * 256, 256), 256)], z_ref[...]).astype(BF16)
-        at = pl.ds(pl.multiple_of(h * 128, 128), 128)
-        by_z[0:512, at] = got[:, :128]
-        by_z[512:1024, at] = got[:, 128:]
+    load(CHUNKS).wait()
+    for chunk in range(CHUNKS):
+        load(chunk).wait()
+
+        @pl.loop(chunk * (16 // CHUNKS), (chunk + 1) * (16 // CHUNKS), unroll=2)
+        def _(h):
+            got = dot(vol_ref[:, pl.ds(pl.multiple_of(h * 256, 256), 256)], z_ref[...]).astype(BF16)
+            at = pl.ds(pl.multiple_of(h * 128, 128), 128)
+            by_z[0:512, at] = got[:, :128]
+            by_z[512:1024, at] = got[:, 128:]
+
+    load(CHUNKS + 1).wait()
 
     @pl.loop(0, 8)
     def _(h2):
@@ -134,6 +202,15 @@
             to = pl.ds(pl.multiple_of(h2 * 64 + i * 32, 32), 32)
             for g in range(16):
                 by_x[to, g * 128 : (g + 1) * 128] = got[g * 32 : (g + 1) * 32, i * 128 : (i + 1) * 128]
+
+    pl.semaphore_wait(barrier, owners - 1)
+
+    @pl.loop(1, owners)
+    def _(k):
+        fact_copy(k).start()
+
+    facts[me] = facts_ref[...]
+    load(CHUNKS + 2).wait()
 
     @pl.loop(0, 8)
     def _(g2):
@@ -144,70 +221,45 @@
             for c in range(2):
                 by_h[:, to, c * 128 : (c + 1) * 128] = got[:, c, :, i * 128 : (i + 1) * 128]
 
-    @pl.loop(0, 16)
+    load(CHUNKS + 3).wait()
+
+    @pl.loop(0, 16, unroll=2)
     def _(q):
         got = dot(by_h[q], y_ref[q])
         for high in range(2):
             spec[pl.ds(high * 16 + q, 256, stride=32), :] = got[:, high * 128 : (high + 1) * 128]
 
+    load(CHUNKS + 4).wait()
     first = lax.broadcasted_iota(jnp.int32, (CELLS // 2, LANES), 1) < LANES // 2
 
-    @pl.loop(0, ROWS)
-    def _(p):
-        own = spec[pl.ds(pl.multiple_of(p * CELLS, CELLS), CELLS), :].astype(BF16)
-        turned = dot(rot_ref[turn_ref[p]], own)
-        factor = dot(left_ref[...], right_ref[:, pl.ds(pl.multiple_of(p * 128, 128), 128)])
-        both = turned * factor
-        wide[...] = both + pltpu.roll(both, LANES // 2, 1)
-        packed = jnp.where(first, wide[pl.ds(0, CELLS // 2, stride=2), :], wide[pl.ds(1, CELLS // 2, stride=2), :])
-        packed = packed.astype(BF16)
-        out_ref[:, p] = packed.reshape(owners, pairs, LANES)
-        long = packed.astype(F32)
-        energy_ref[pl.ds(p, 1), :] = jnp.sum(long * long, axis=0, keepdims=True)
-
-
-def classes(owners, send_ref, facts_ref, energy_ref, refs_ref, new_ref, score_ref,
-            held, facts, wide, chosen, below, parts, answer, sems):
-    me = lax.axis_index("dev")
-    class_count, columns = refs_ref.shape
-    pairs = columns // LANES
-    particles = owners * ROWS
-
-    def copy(i, k):
-        to = lax.rem(me + k, owners)
-        src = (facts_ref, send_ref.at[to], parts.at[to])[i]
-        dst = (facts, held, answer)[i]
-        return pltpu.make_async_remote_copy(
-            src_ref=src, dst_ref=dst.at[me],
-            send_sem=sems.at[2 * i, k], recv_sem=sems.at[2 * i + 1, k],
-            device_id={"dev": to}, device_id_type=pl.DeviceIdType.MESH,
-        )
-
-    barrier = pltpu.get_barrier_semaphore()
-
-    @pl.loop(1, owners)
-    def _(k):
-        pl.semaphore_signal(
-            barrier, inc=1, device_id={"dev": lax.rem(me + k, owners)}, device_id_type=pl.DeviceIdType.MESH
-        )
-
-    pl.semaphore_wait(barrier, owners - 1)
-
-    @pl.loop(1, owners)
-    def _(k):
-        copy(0, k).start()
-
-    @pl.loop(1, owners)
-    def _(k):
-        copy(1, k).start()
-
-    facts[me] = facts_ref[...]
-    held[me] = send_ref[me]
-
-    @pl.loop(1, owners)
-    def _(k):
-        copy(0, k).wait()
-
+    @pl.loop(0, ROWS // GROUP)
+    def _(g):
+        @pl.loop(0, GROUP)
+        def _(within):
+            p = g * GROUP + within
+            own = spec[pl.ds(pl.multiple_of(p * CELLS, CELLS), CELLS), :].astype(BF16)
+            turned = dot(rot_ref[turn_ref[p]], own)
+            factor = dot(left_ref[...], right_ref[:, pl.ds(pl.multiple_of(p * 128, 128), 128)])
+            both = turned * factor
+            wide[0:CELLS, :] = both + pltpu.roll(both, LANES // 2, 1)
+            even = wide[pl.ds(0, CELLS // 2, stride=2), :]
+            odd = wide[pl.ds(1, CELLS // 2, stride=2), :]
+            packed = jnp.where(first, even, odd).astype(BF16)
+            send[:, p] = packed.reshape(owners, pairs, LANES)
+            long = packed.astype(F32)
+            energy_ref[pl.ds(p, 1), :] = jnp.sum(long * long, axis=0, keepdims=True)
+
+        @pl.loop(1, owners)
+        def _(k):
+            data_copy(g, k).start()
+
+    held[me] = send[me]
+
+    @pl.loop(1, owners)
+    def _(k):
+        fact_copy(k).wait()
+
+    load(CHUNKS + 5).wait()
     known = facts[...].reshape(particles, LANES)
     lane = lax.broadcasted_iota(jnp.int32, (particles, LANES), 1)
     member = jnp.where(known[:, 0:1] == lane.astype(F32), 1.0, 0.0)
@@ -216,7 +268,7 @@
     one = lax.broadcasted_iota(jnp.int32, (1, LANES), 1)
     kz = one % BAND - BAND // 2
 
-    @pl.loop(0, pairs)
+    @pl.loop(0, pairs, unroll=2)
     def _(r):
         cell = (me * pairs + r) * 2 + one // (2 * BAND)
         kx = cell // BAND - BAND // 2
@@ -228,14 +280,16 @@
         at = pl.ds(pl.multiple_of(r * LANES, LANES), LANES)
         chosen[r] = dot(member[:, :class_count].astype(BF16), refs_ref[:, at])
 
-    @pl.loop(1, owners)
-    def _(k):
-        copy(1, k).wait()
-
-    wide[...] = held[...].astype(F32).reshape(particles * pairs, LANES)
+    @pl.loop(0, ROWS // GROUP)
+    def _(g):
+        @pl.loop(1, owners)
+        def _(k):
+            data_copy(g, k).wait()
+
+    wide[0 : particles * pairs, :] = held[...].astype(F32).reshape(particles * pairs, LANES)
     parts[...] = jnp.zeros_like(parts)
 
-    @pl.loop(0, pairs)
+    @pl.loop(0, pairs, unroll=4)
     def _(r):
         rows = wide[pl.ds(r, particles, stride=pairs), :]
         total = dot(across.astype(BF16), rows.astype(BF16))
@@ -244,13 +298,13 @@
 
     @pl.loop(1, owners)
     def _(k):
-        copy(2, k).start()
+        answer_copy(k).start()
 
     answer[me] = parts[me]
 
     @pl.loop(1, owners)
     def _(k):
-        copy(2, k).wait()
+        answer_copy(k).wait()
 
     agreement = jnp.sum(jnp.sum(answer[...], axis=0), axis=1, keepdims=True)
     energy = jnp.sum(energy_ref[...], axis=1, keepdims=True)
@@ -261,51 +315,44 @@
     class_count, columns = references.shape
     pairs = columns // LANES
     particles = owners * ROWS
-    facts = jnp.concatenate(
-        [labels.astype(F32)[:, None], defocus[:, None], shifts.astype(F32), jnp.zeros((ROWS, LANES - 5), F32)], axis=1
-    )
     rows = volumes.reshape(ROWS, BOX, BOX * BOX).transpose(1, 0, 2).reshape(BOX * ROWS, BOX * BOX)
-    send, energy = pl.pallas_call(
-        spectra,
+    constants = [jnp.asarray(t) for t in tables()]
+    new_refs, scores = pl.pallas_call(
+        lambda *refs: whole(owners, *refs),
         out_shape=(
-            jax.ShapeDtypeStruct((owners, ROWS, pairs, LANES), BF16),
+            jax.ShapeDtypeStruct((class_count, columns), F32),
             jax.ShapeDtypeStruct((ROWS, LANES), F32),
         ),
-        in_specs=[SMEM] + [VMEM] * 7,
+        in_specs=[SMEM] * 4 + [HBM] * 7,
         out_specs=(VMEM, VMEM),
         scratch_shapes=[
+            pltpu.VMEM(x.shape, BF16) for x in (rows, rotations, references, *constants)
+        ] + [
             pltpu.VMEM((1024, 2048), BF16),
             pltpu.VMEM((512, 2048), BF16),
             pltpu.VMEM((16, 256, 256), BF16),
             pltpu.VMEM((ROWS * CELLS, LANES), F32),
             pltpu.VMEM((CELLS, LANES), BF16),
             pltpu.VMEM((LANES, ROWS * LANES), BF16),
-            pltpu.VMEM((CELLS, LANES), F32),
-        ],
-        compiler_params=pltpu.CompilerParams(vmem_limit_bytes=48 * 1024 * 1024),
-    )(turn_ids, rows, rotations, facts, *(jnp.asarray(t) for t in tables()))
-    new_refs, scores = pl.pallas_call(
-        lambda *refs: classes(owners, *refs),
-        out_shape=(
-            jax.ShapeDtypeStruct((class_count, columns), F32),
-            jax.ShapeDtypeStruct((ROWS, LANES), F32),
-        ),
-        in_specs=[VMEM] * 4,
-        out_specs=(VMEM, VMEM),
-        scratch_shapes=[
+            pltpu.VMEM((max(CELLS, particles * pairs), LANES), F32),
+            pltpu.VMEM((ROWS, LANES), F32),
             pltpu.VMEM((owners, ROWS, pairs, LANES), BF16),
+            pltpu.VMEM((owners, ROWS, pairs, LANES), BF16),
+            pltpu.VMEM((ROWS, LANES), F32),
             pltpu.VMEM((owners, ROWS, LANES), F32),
-            pltpu.VMEM((particles * pairs, LANES), F32),
             pltpu.VMEM((pairs, particles, LANES), F32),
             pltpu.VMEM((pairs, class_count, LANES), F32),
             pltpu.VMEM((owners, ROWS, LANES), F32),
             pltpu.VMEM((owners, ROWS, LANES), F32),
-            pltpu.SemaphoreType.DMA((6, owners)),
+            pltpu.SemaphoreType.DMA((CHUNKS + 6,)),
+            pltpu.SemaphoreType.DMA((2, owners)),
+            pltpu.SemaphoreType.DMA((ROWS // GROUP, 2, owners)),
+            pltpu.SemaphoreType.DMA((2, owners)),
         ],
         compiler_params=pltpu.CompilerParams(
-            collective_id=0, has_side_effects=True, vmem_limit_bytes=48 * 1024 * 1024
+            collective_id=0, has_side_effects=True, vmem_limit_bytes=52 * 1024 * 1024
         ),
-    )(send, facts, energy, references)
+    )(turn_ids, labels, defocus, shifts.T, rows, rotations, references, *constants)
     return new_refs, scores[:, 0]
 
 

time: 85.3 us -> 60.6 us (0.71)
  Pallas kernels: 75 us -> 52.5 us
  local copies, waits for them, and re-layouts: 8.57 us -> 7.09 us
    pallas_call x2 -> x1, Pallas kernels: 75 us -> 52.5 us  [on_device(): pl.pallas_call(lambda *refs: whole(owners, *refs), out_shape=(jax.ShapeDt...]
    unnamed x14 -> x15, local copies, waits for them, and re-layouts: 7.05 us -> 6.46 us
where the time goes in v3:
time: 60.6 us; the launch traced here: 60.3 us
  Pallas kernels  52.5 us (87%)
  local copies, waits for them, and re-layouts  7.09 us (12%)
  between operations  0.66 us (1%)
    pallas_call x1, Pallas kernels, on_device(): pl.pallas_call(lambda *refs: whole(owners, *refs), out_shape=(jax.ShapeDt...  52.5 us
    unnamed x15, local copies, waits for them, and re-layouts  6.46 us

profile of v3, /device:TPU:0, one launch (start us, length us, event | category | flops | bytes accessed | tf_op | source)
XLA Modules:
  0.0 60.3 jit_solution(15127821395120780346)
XLA Ops:
  0.6 0.0 copy-start
  0.6 1.0 %copy-done = bf16[512,512]{1,0:T(8,128)(2,1)S(1)} copy-done((bf16[512,512]{1,0:T(8,128)(2,1)S(1)}, bf16[512,512]{1,0:T(8,128)(2,1)}, u32[]{:S(2)}) %copy-start) | copy-done | bytes 524312
  1.7 0.0 copy-start.1
  1.7 1.0 %copy-done.1 = bf16[48,4096]{1,0:T(8,128)(2,1)S(1)} copy-done((bf16[48,4096]{1,0:T(8,128)(2,1)S(1)}, bf16[48,4096]{1,0:T(8,128)(2,1)}, u32[]{:S(2)}) %copy-start.1) | copy-done | bytes 393240
  2.7 0.0 copy-start.2
  2.7 0.9 %copy-done.2 = bf16[256,256]{1,0:T(8,128)(2,1)S(1)} copy-done((bf16[256,256]{1,0:T(8,128)(2,1)S(1)}, bf16[256,256]{1,0:T(8,128)(2,1)}, u32[]{:S(2)}) %copy-start.2) | copy-done | bytes 131096
  3.6 0.0 copy-start.3
  3.6 0.7 %copy-done.3 = s32[8,3]{0,1:T(4,128)S(1)} copy-done((s32[8,3]{0,1:T(4,128)S(1)}, s32[8,3]{0,1:T(4,128)}, u32[]{:S(2)}) %copy-start.3) | copy-done | bytes 120
  4.3 0.0 copy-start.4
  4.3 0.7 %copy-done.4 = s32[8]{0:T(128)S(1)} copy-done((s32[8]{0:T(128)S(1)}, s32[8]{0:T(128)}, u32[]{:S(2)}) %copy-start.4) | copy-done | bytes 56
  4.9 0.0 copy-start.5
  4.9 0.7 %copy-done.5 = s32[8]{0:T(128)S(1)} copy-done((s32[8]{0:T(128)S(1)}, s32[8]{0:T(128)}, u32[]{:S(2)}) %copy-start.5) | copy-done | bytes 56
  5.6 0.0 copy-start.6
  5.6 0.7 %copy-done.6 = f32[8]{0:T(128)S(1)} copy-done((f32[8]{0:T(128)S(1)}, f32[8]{0:T(128)}, u32[]{:S(2)}) %copy-start.6) | copy-done | bytes 56
  6.2 52.5 %shard_map.122 = (f32[48,4096]{1,0:T(8,128)S(1)}, f32[8,128]{1,0:T(8,128)S(1)}) custom-call(s32[8]{0:T(128)S(1)} %copy-done.4, s32[8]{0:T(128)S(1)} %copy-done.5, f32[8]{0:T(128)S(1)} %copy-done.6, s32[3,8]{1,0:T(4,128)S(1)} %bitcast.6, bf16[512,4096]{1,0:T(8,128)(2,1)} %bitcast.7, bf16[3,1024,1024]{2,1,0:T(8,128)(2,1)} %refs_5_.1, ...), custom_call_target="tpu_custom_call" | custom-call | tf_op jit(solution)/shard_map/pallas_call | solution.py:320
  58.8 0.6 %slice_reduce_fusion = f32[8]{0:T(128)} fusion(f32[8,128]{1,0:T(8,128)S(1)} %get-tuple-element.5), kind=kLoop, calls=%fused_computation | loop fusion | bytes 64 | tf_op jit(solution)/shard_map/slice | solution.py:356
  59.4 0.9 %copy.14 = f32[48,4096]{1,0:T(8,128)} copy(f32[48,4096]{1,0:T(8,128)S(1)} %get-tuple-element.8) | data formatting | bytes 1572864
Async XLA Ops:
  0.6 1.0 %copy-start = (bf16[512,512]{1,0:T(8,128)(2,1)S(1)}, bf16[512,512]{1,0:T(8,128)(2,1)}, u32[]{:S(2)}) copy-start(bf16[512,512]{1,0:T(8,128)(2,1)} %constant.10.clone.refs_9_) | copy-start | bytes 1572868
  1.7 1.0 %copy-start.1 = (bf16[48,4096]{1,0:T(8,128)(2,1)S(1)}, bf16[48,4096]{1,0:T(8,128)(2,1)}, u32[]{:S(2)}) copy-start(bf16[48,4096]{1,0:T(8,128)(2,1)} %refs_6_.1) | copy-start | bytes 1179652
  2.7 0.9 %copy-start.2 = (bf16[256,256]{1,0:T(8,128)(2,1)S(1)}, bf16[256,256]{1,0:T(8,128)(2,1)}, u32[]{:S(2)}) copy-start(bf16[256,256]{1,0:T(8,128)(2,1)} %constant.8.clone.refs_7_) | copy-start | bytes 393220
  3.6 0.7 %copy-start.3 = (s32[8,3]{0,1:T(4,128)S(1)}, s32[8,3]{0,1:T(4,128)}, u32[]{:S(2)}) copy-start(s32[8,3]{0,1:T(4,128)} %param.14) | copy-start | bytes 292
  4.3 0.7 %copy-start.4 = (s32[8]{0:T(128)S(1)}, s32[8]{0:T(128)}, u32[]{:S(2)}) copy-start(s32[8]{0:T(128)} %refs_0_.1) | copy-start | bytes 100
  4.9 0.7 %copy-start.5 = (s32[8]{0:T(128)S(1)}, s32[8]{0:T(128)}, u32[]{:S(2)}) copy-start(s32[8]{0:T(128)} %refs_1_.1) | copy-start | bytes 100
  5.6 0.7 %copy-start.6 = (f32[8]{0:T(128)S(1)}, f32[8]{0:T(128)}, u32[]{:S(2)}) copy-start(f32[8]{0:T(128)} %refs_2_.1) | copy-start | bytes 100

commit v4 on v3

--- a/solution.py
+++ b/solution.py
@@ -16,6 +16,8 @@
 LANES = 128
 CHUNKS = 4
 GROUP = 2
+STEPS = 4
+STEP = ROWS // STEPS
 TWO_PI = 2.0 * math.pi
 VMEM = pl.BlockSpec(memory_space=pltpu.VMEM)
 HBM = pl.BlockSpec(memory_space=pltpu.HBM)
@@ -25,7 +27,8 @@
 
 
 def rounded(table):
-    return np.asarray(table, np.float32).astype(ml_dtypes.bfloat16)
+    table = np.asarray(table, np.float32).astype(ml_dtypes.bfloat16)
+    return table.reshape(*table.shape[:-2], -1, 8, table.shape[-1])
 
 
 def tables():
@@ -188,16 +191,16 @@
 
         @pl.loop(chunk * (16 // CHUNKS), (chunk + 1) * (16 // CHUNKS), unroll=2)
         def _(h):
-            got = dot(vol_ref[:, pl.ds(pl.multiple_of(h * 256, 256), 256)], z_ref[...]).astype(BF16)
+            got = dot(vol_ref[:, pl.ds(pl.multiple_of(h * 256, 256), 256)], z_ref[...].reshape(256, 256)).astype(BF16)
             at = pl.ds(pl.multiple_of(h * 128, 128), 128)
             by_z[0:512, at] = got[:, :128]
             by_z[512:1024, at] = got[:, 128:]
 
     load(CHUNKS + 1).wait()
 
-    @pl.loop(0, 8)
+    @pl.loop(0, 8, unroll=2)
     def _(h2):
-        got = dot(x_ref[...], by_z[:, pl.ds(pl.multiple_of(h2 * 256, 256), 256)]).astype(BF16)
+        got = dot(x_ref[...].reshape(512, 1024), by_z[:, pl.ds(pl.multiple_of(h2 * 256, 256), 256)]).astype(BF16)
         for i in range(2):
             to = pl.ds(pl.multiple_of(h2 * 64 + i * 32, 32), 32)
             for g in range(16):
@@ -210,48 +213,50 @@
         fact_copy(k).start()
 
     facts[me] = facts_ref[...]
-    load(CHUNKS + 2).wait()
-
-    @pl.loop(0, 8)
-    def _(g2):
-        got = dot(h_ref[...], by_x[:, pl.ds(pl.multiple_of(g2 * 256, 256), 256)]).astype(BF16)
-        got = got.reshape(16, 2, 16, 256)
-        for i in range(2):
-            to = pl.ds(pl.multiple_of(g2 * 32 + i * 16, 16), 16)
-            for c in range(2):
-                by_h[:, to, c * 128 : (c + 1) * 128] = got[:, c, :, i * 128 : (i + 1) * 128]
-
-    load(CHUNKS + 3).wait()
-
-    @pl.loop(0, 16, unroll=2)
-    def _(q):
-        got = dot(by_h[q], y_ref[q])
-        for high in range(2):
-            spec[pl.ds(high * 16 + q, 256, stride=32), :] = got[:, high * 128 : (high + 1) * 128]
-
-    load(CHUNKS + 4).wait()
     first = lax.broadcasted_iota(jnp.int32, (CELLS // 2, LANES), 1) < LANES // 2
-
-    @pl.loop(0, ROWS // GROUP)
-    def _(g):
-        @pl.loop(0, GROUP)
+    for i in (2, 3, 4):
+        load(CHUNKS + i).wait()
+
+    @pl.loop(0, STEPS)
+    def _(step):
+        @pl.loop(0, STEP, unroll=min(STEP, 2))
         def _(within):
-            p = g * GROUP + within
-            own = spec[pl.ds(pl.multiple_of(p * CELLS, CELLS), CELLS), :].astype(BF16)
-            turned = dot(rot_ref[turn_ref[p]], own)
-            factor = dot(left_ref[...], right_ref[:, pl.ds(pl.multiple_of(p * 128, 128), 128)])
-            both = turned * factor
-            wide[0:CELLS, :] = both + pltpu.roll(both, LANES // 2, 1)
-            even = wide[pl.ds(0, CELLS // 2, stride=2), :]
-            odd = wide[pl.ds(1, CELLS // 2, stride=2), :]
-            packed = jnp.where(first, even, odd).astype(BF16)
-            send[:, p] = packed.reshape(owners, pairs, LANES)
-            long = packed.astype(F32)
-            energy_ref[pl.ds(p, 1), :] = jnp.sum(long * long, axis=0, keepdims=True)
-
-        @pl.loop(1, owners)
-        def _(k):
-            data_copy(g, k).start()
+            p = step * STEP + within
+            got = dot(h_ref[...].reshape(512, 512), by_x[:, pl.ds(pl.multiple_of(p * 256, 256), 256)]).astype(BF16)
+            got = got.reshape(16, 2, 16, 256)
+            for i in range(2):
+                to = pl.ds(pl.multiple_of(p * 32 + i * 16, 16), 16)
+                for c in range(2):
+                    by_h[:, to, c * 128 : (c + 1) * 128] = got[:, c, :, i * 128 : (i + 1) * 128]
+
+        @pl.loop(0, 16, unroll=4)
+        def _(q):
+            own = by_h[q, pl.ds(pl.multiple_of(step * STEP * 32, STEP * 32), STEP * 32), :]
+            got = dot(own, y_ref[q].reshape(256, 256))
+            for high in range(2):
+                to = pl.ds(step * STEP * CELLS + high * 16 + q, STEP * 32, stride=32)
+                spec[to, :] = got[:, high * 128 : (high + 1) * 128]
+
+        @pl.loop(step * (STEP // GROUP), (step + 1) * (STEP // GROUP))
+        def _(g):
+            @pl.loop(0, GROUP)
+            def _(within):
+                p = g * GROUP + within
+                own = spec[pl.ds(pl.multiple_of(p * CELLS, CELLS), CELLS), :].astype(BF16)
+                turned = dot(rot_ref[turn_ref[p]], own)
+                factor = dot(left_ref[...], right_ref[:, pl.ds(pl.multiple_of(p * 128, 128), 128)])
+                both = turned * factor
+                wide[0:CELLS, :] = both + pltpu.roll(both, LANES // 2, 1)
+                even = wide[pl.ds(0, CELLS // 2, stride=2), :]
+                odd = wide[pl.ds(1, CELLS // 2, stride=2), :]
+                packed = jnp.where(first, even, odd).astype(BF16)
+                send[:, p] = packed.reshape(owners, pairs, LANES)
+                long = packed.astype(F32)
+                energy_ref[pl.ds(p, 1), :] = jnp.sum(long * long, axis=0, keepdims=True)
+
+            @pl.loop(1, owners)
+            def _(k):
+                data_copy(g, k).start()
 
     held[me] = send[me]
 
@@ -292,15 +297,19 @@
     @pl.loop(0, pairs, unroll=4)
     def _(r):
         rows = wide[pl.ds(r, particles, stride=pairs), :]
+        parts[...] += (rows * chosen[r]).reshape(owners, ROWS, LANES)
+
+    @pl.loop(1, owners)
+    def _(k):
+        answer_copy(k).start()
+
+    answer[me] = parts[me]
+
+    @pl.loop(0, pairs, unroll=4)
+    def _(r):
+        rows = wide[pl.ds(r, particles, stride=pairs), :]
         total = dot(across.astype(BF16), rows.astype(BF16))
         new_ref[:, pl.ds(pl.multiple_of(r * LANES, LANES), LANES)] = total * below[r]
-        parts[...] += (rows * chosen[r]).reshape(owners, ROWS, LANES)
-
-    @pl.loop(1, owners)
-    def _(k):
-        answer_copy(k).start()
-
-    answer[me] = parts[me]
 
     @pl.loop(1, owners)
     def _(k):
@@ -350,7 +359,7 @@
             pltpu.SemaphoreType.DMA((2, owners)),
         ],
         compiler_params=pltpu.CompilerParams(
-            collective_id=0, has_side_effects=True, vmem_limit_bytes=52 * 1024 * 1024
+            collective_id=0, has_side_effects=True, vmem_limit_bytes=64 * 1024 * 1024
         ),
     )(turn_ids, labels, defocus, shifts.T, rows, rotations, references, *constants)
     return new_refs, scores[:, 0]

time: 60.6 us -> 53.1 us (0.88)
  local copies, waits for them, and re-layouts: 7.09 us -> 3.36 us
  Pallas kernels: 52.5 us -> 48.9 us
    unnamed x15 -> x1, local copies, waits for them, and re-layouts: 6.46 us -> 2.06 us
    pallas_call x1, Pallas kernels: 52.5 us -> 48.9 us  [on_device(): pl.pallas_call(lambda *refs: whole(owners, *refs), out_shape=(jax.ShapeDt...]
    slice x1, local copies, waits for them, and re-layouts: 0.63 us -> 1.3 us  [on_device(): return (new_refs, scores[:, 0])]
where the time goes in v4:
time: 53.1 us; the launch traced here: 52.9 us
  Pallas kernels  48.9 us (92%)
  local copies, waits for them, and re-layouts  3.36 us (6%)
  between operations  0.64 us (1%)
    pallas_call x1, Pallas kernels, on_device(): pl.pallas_call(lambda *refs: whole(owners, *refs), out_shape=(jax.ShapeDt...  48.9 us
    unnamed x1, local copies, waits for them, and re-layouts  2.06 us
    slice x1, local copies, waits for them, and re-layouts, on_device(): return (new_refs, scores[:, 0])  1.3 us

profile of v4, /device:TPU:0, one launch (start us, length us, event | category | flops | bytes accessed | tf_op | source)
XLA Modules:
  0.0 52.9 jit_solution(17095306755722973598)
XLA Ops:
  0.6 48.9 %shard_map.122 = (f32[48,4096]{1,0:T(8,128)}, f32[8,128]{1,0:T(8,128)}) custom-call(s32[8]{0:T(128)} %refs_0_.1, s32[8]{0:T(128)} %refs_1_.1, f32[8]{0:T(128)} %refs_2_.1, s32[3,8]{1,0:T(4,128)} %bitcast.7, bf16[512,4096]{1,0:T(8,128)(2,1)} %bitcast.6, bf16[3,1024,1024]{2,1,0:T(8,128)(2,1)} %refs_5_.1, bf16[48,4096]{1,0:T(8,128)(2,1)} %refs_6_.1, ...), custom_call_target="tpu_custom_call" | custom-call | tf_op jit(solution)/shard_map/pallas_call | solution.py:329
  49.5 1.3 %slice_reduce_fusion = f32[8]{0:T(128)} fusion(f32[8,128]{1,0:T(8,128)} %get-tuple-element.5), kind=kLoop, calls=%fused_computation | loop fusion | bytes 64 | tf_op jit(solution)/shard_map/slice | solution.py:365
  50.8 2.1 %copy.14 = f32[48,4096]{1,0:T(8,128)} copy(f32[48,4096]{1,0:T(8,128)} %get-tuple-element.8) | data formatting | bytes 1572864

commit v5 on v4

--- a/solution.py
+++ b/solution.py
@@ -14,7 +14,7 @@
 ROWS = 8
 CELLS = BAND * BAND
 LANES = 128
-CHUNKS = 4
+CHUNKS = 8
 GROUP = 2
 STEPS = 4
 STEP = ROWS // STEPS
@@ -198,7 +198,7 @@
 
     load(CHUNKS + 1).wait()
 
-    @pl.loop(0, 8, unroll=2)
+    @pl.loop(0, 8, unroll=4)
     def _(h2):
         got = dot(x_ref[...].reshape(512, 1024), by_z[:, pl.ds(pl.multiple_of(h2 * 256, 256), 256)]).astype(BF16)
         for i in range(2):
@@ -229,7 +229,7 @@
                 for c in range(2):
                     by_h[:, to, c * 128 : (c + 1) * 128] = got[:, c, :, i * 128 : (i + 1) * 128]
 
-        @pl.loop(0, 16, unroll=4)
+        @pl.loop(0, 16, unroll=8)
         def _(q):
             own = by_h[q, pl.ds(pl.multiple_of(step * STEP * 32, STEP * 32), STEP * 32), :]
             got = dot(own, y_ref[q].reshape(256, 256))
@@ -239,16 +239,17 @@
 
         @pl.loop(step * (STEP // GROUP), (step + 1) * (STEP // GROUP))
         def _(g):
-            @pl.loop(0, GROUP)
+            @pl.loop(0, GROUP, unroll=GROUP)
             def _(within):
                 p = g * GROUP + within
                 own = spec[pl.ds(pl.multiple_of(p * CELLS, CELLS), CELLS), :].astype(BF16)
                 turned = dot(rot_ref[turn_ref[p]], own)
                 factor = dot(left_ref[...], right_ref[:, pl.ds(pl.multiple_of(p * 128, 128), 128)])
                 both = turned * factor
-                wide[0:CELLS, :] = both + pltpu.roll(both, LANES // 2, 1)
-                even = wide[pl.ds(0, CELLS // 2, stride=2), :]
-                odd = wide[pl.ds(1, CELLS // 2, stride=2), :]
+                at = within * CELLS
+                wide[pl.ds(pl.multiple_of(at, CELLS), CELLS), :] = both + pltpu.roll(both, LANES // 2, 1)
+                even = wide[pl.ds(at, CELLS // 2, stride=2), :]
+                odd = wide[pl.ds(at + 1, CELLS // 2, stride=2), :]
                 packed = jnp.where(first, even, odd).astype(BF16)
                 send[:, p] = packed.reshape(owners, pairs, LANES)
                 long = packed.astype(F32)
@@ -273,17 +274,26 @@
     one = lax.broadcasted_iota(jnp.int32, (1, LANES), 1)
     kz = one % BAND - BAND // 2
 
-    @pl.loop(0, pairs, unroll=2)
-    def _(r):
-        cell = (me * pairs + r) * 2 + one // (2 * BAND)
+    across = across.astype(BF16)
+    quarter = lax.broadcasted_iota(jnp.int32, (class_count, LANES), 1) // BAND
+
+    @pl.loop(0, pairs // 2, unroll=2)
+    def _(r2):
+        cell = (me * pairs + r2 * 2) * 2 + one // BAND
         kx = cell // BAND - BAND // 2
         ky = cell % BAND - BAND // 2
         radius = (kx * kx + ky * ky + kz * kz).astype(F32)
         weight = jnp.sin(defocus * radius / BAND + 0.3)
-        total = jnp.dot(across, weight * weight, preferred_element_type=F32, precision=lax.Precision.HIGHEST)
-        below[r] = 1.0 / (total + 1.0)
-        at = pl.ds(pl.multiple_of(r * LANES, LANES), LANES)
-        chosen[r] = dot(member[:, :class_count].astype(BF16), refs_ref[:, at])
+        high, low = halves(weight * weight)
+        total = dot(across, high.astype(BF16)) + dot(across, low.astype(BF16))
+        total = 1.0 / (total + 1.0)
+        by_one, by_two, by_three = (pltpu.roll(total, i * BAND, 1) for i in (1, 2, 3))
+        below[r2 * 2] = jnp.where(quarter == 0, total, jnp.where(quarter == 3, by_two, by_one))
+        below[r2 * 2 + 1] = jnp.where(quarter == 3, total, jnp.where(quarter == 0, by_two, by_three))
+        for i in range(2):
+            r = r2 * 2 + i
+            at = pl.ds(pl.multiple_of(r * LANES, LANES), LANES)
+            chosen[r] = dot(member[:, :class_count].astype(BF16), refs_ref[:, at])
 
     @pl.loop(0, ROWS // GROUP)
     def _(g):
@@ -308,7 +318,7 @@
     @pl.loop(0, pairs, unroll=4)
     def _(r):
         rows = wide[pl.ds(r, particles, stride=pairs), :]
-        total = dot(across.astype(BF16), rows.astype(BF16))
+        total = dot(across, rows.astype(BF16))
         new_ref[:, pl.ds(pl.multiple_of(r * LANES, LANES), LANES)] = total * below[r]
 
     @pl.loop(1, owners)
@@ -343,7 +353,7 @@
             pltpu.VMEM((ROWS * CELLS, LANES), F32),
             pltpu.VMEM((CELLS, LANES), BF16),
             pltpu.VMEM((LANES, ROWS * LANES), BF16),
-            pltpu.VMEM((max(CELLS, particles * pairs), LANES), F32),
+            pltpu.VMEM((max(GROUP * CELLS, particles * pairs), LANES), F32),
             pltpu.VMEM((ROWS, LANES), F32),
             pltpu.VMEM((owners, ROWS, pairs, LANES), BF16),
             pltpu.VMEM((owners, ROWS, pairs, LANES), BF16),

time: 53.1 us -> 50.6 us (0.953)
  Pallas kernels: 48.9 us -> 46.4 us
    pallas_call x1, Pallas kernels: 48.9 us -> 46.4 us  [on_device(): pl.pallas_call(lambda *refs: whole(owners, *refs), out_shape=(jax.ShapeDt...]
where the time goes in v5:
time: 50.6 us; the launch traced here: 50.4 us
  Pallas kernels  46.4 us (92%)
  local copies, waits for them, and re-layouts  3.36 us (7%)
  between operations  0.64 us (1%)
    pallas_call x1, Pallas kernels, on_device(): pl.pallas_call(lambda *refs: whole(owners, *refs), out_shape=(jax.ShapeDt...  46.4 us
    unnamed x1, local copies, waits for them, and re-layouts  2.06 us
    slice x1, local copies, waits for them, and re-layouts, on_device(): return (new_refs, scores[:, 0])  1.3 us

profile of v5, /device:TPU:0, one launch (start us, length us, event | category | flops | bytes accessed | tf_op | source)
XLA Modules:
  0.0 50.4 jit_solution(13716631727580102514)
XLA Ops:
  0.6 46.4 %shard_map.122 = (f32[48,4096]{1,0:T(8,128)}, f32[8,128]{1,0:T(8,128)}) custom-call(s32[8]{0:T(128)} %refs_0_.1, s32[8]{0:T(128)} %refs_1_.1, f32[8]{0:T(128)} %refs_2_.1, s32[3,8]{1,0:T(4,128)} %bitcast.7, bf16[512,4096]{1,0:T(8,128)(2,1)} %bitcast.6, bf16[3,1024,1024]{2,1,0:T(8,128)(2,1)} %refs_5_.1, bf16[48,4096]{1,0:T(8,128)(2,1)} %refs_6_.1, ...), custom_call_target="tpu_custom_call" | custom-call | tf_op jit(solution)/shard_map/pallas_call | solution.py:339
  47.0 1.3 %slice_reduce_fusion = f32[8]{0:T(128)} fusion(f32[8,128]{1,0:T(8,128)} %get-tuple-element.5), kind=kLoop, calls=%fused_computation | loop fusion | bytes 64 | tf_op jit(solution)/shard_map/slice | solution.py:375
  48.3 2.1 %copy.14 = f32[48,4096]{1,0:T(8,128)} copy(f32[48,4096]{1,0:T(8,128)} %get-tuple-element.8) | data formatting | bytes 1572864

commit v6 on v5

--- a/solution.py
+++ b/solution.py
@@ -327,7 +327,8 @@
 
     agreement = jnp.sum(jnp.sum(answer[...], axis=0), axis=1, keepdims=True)
     energy = jnp.sum(energy_ref[...], axis=1, keepdims=True)
-    score_ref[...] = jnp.broadcast_to(agreement / jnp.sqrt(energy + 1e-06), (ROWS, LANES))
+    score = jnp.broadcast_to(agreement / jnp.sqrt(energy + 1e-06), (ROWS, LANES))
+    score_ref[...] = score.T[0:1]
 
 
 def on_device(owners, volumes, rotations, turn_ids, shifts, defocus, labels, references):
@@ -340,7 +341,7 @@
         lambda *refs: whole(owners, *refs),
         out_shape=(
             jax.ShapeDtypeStruct((class_count, columns), F32),
-            jax.ShapeDtypeStruct((ROWS, LANES), F32),
+            jax.ShapeDtypeStruct((1, ROWS), F32),
         ),
         in_specs=[SMEM] * 4 + [HBM] * 7,
         out_specs=(VMEM, VMEM),
@@ -372,7 +373,7 @@
             collective_id=0, has_side_effects=True, vmem_limit_bytes=64 * 1024 * 1024
         ),
     )(turn_ids, labels, defocus, shifts.T, rows, rotations, references, *constants)
-    return new_refs, scores[:, 0]
+    return new_refs, scores[0]
 
 
 def solution(mesh):

time: 50.6 us -> 50.4 us (level)
    slice x1 -> x0, local copies, waits for them, and re-layouts: 1.3 us -> none  [on_device(): return (new_refs, scores[:, 0])]
    unnamed x1 -> x2, local copies, waits for them, and re-layouts: 2.06 us -> 3.15 us
where the time goes in v6:
time: 50.4 us; the launch traced here: 50.2 us
  Pallas kernels  46.4 us (92%)
  local copies, waits for them, and re-layouts  3.15 us (6%)
  between operations  0.64 us (1%)
    pallas_call x1, Pallas kernels, on_device(): pl.pallas_call(lambda *refs: whole(owners, *refs), out_shape=(jax.ShapeDt...  46.4 us
    unnamed x2, local copies, waits for them, and re-layouts  3.15 us

profile of v6, /device:TPU:0, one launch (start us, length us, event | category | flops | bytes accessed | tf_op | source)
XLA Modules:
  0.0 50.2 jit_solution(17261779389516654679)
XLA Ops:
  0.6 46.4 %shard_map.122 = (f32[48,4096]{1,0:T(8,128)}, f32[1,8]{1,0:T(1,128)}) custom-call(s32[8]{0:T(128)} %refs_0_.1, s32[8]{0:T(128)} %refs_1_.1, f32[8]{0:T(128)} %refs_2_.1, s32[3,8]{1,0:T(4,128)} %bitcast.8, bf16[512,4096]{1,0:T(8,128)(2,1)} %bitcast.7, bf16[3,1024,1024]{2,1,0:T(8,128)(2,1)} %refs_5_.1, bf16[48,4096]{1,0:T(8,128)(2,1)} %refs_6_.1, ...), custom_call_target="tpu_custom_call" | custom-call | tf_op jit(solution)/shard_map/pallas_call | solution.py:340
  47.1 2.1 %copy.15 = f32[48,4096]{1,0:T(8,128)} copy(f32[48,4096]{1,0:T(8,128)} %get-tuple-element.8) | data formatting | bytes 1572864
  49.1 1.1 %copy.16 = f32[8]{0:T(128)} copy(f32[8]{0:T(128)} %bitcast.9) | data formatting | bytes 64
